TPU v7x, 256 devices: a whole 4x4x8 slice. The times are simulated.
256 devices in a mesh: region: 64 (over y, x_hi, z), station: 4 (over x_lo, core).
Axes of the slice: x: 4 (x_hi: 2, x_lo: 2; x = x_hi * 2 + x_lo), y: 4, z: 8, core: 2. Of those that a mesh axis runs over, the one named last changes fastest.
Arguments:
- waveforms: bfloat16 [1024, 16, 3, 512], P('region', 'station'), may hold values from -6 to 6
- pair_lists: int32 [3, 2048, 2], P(None, 'region'), may hold values from 0 to 15
- pair_counts: int32 [3, 64], P(None, 'region'), may hold values from 1 to 32, as said below
Outputs:
- correlations: float32 [3, 2048, 256], P(None, ('region', 'station'))
Inputs may be any that keep to these rules, and one draw needn't show every extreme that they name: `pair_counts`: in every round some region has all 32 slots live.
All inputs are finite; a program needn't handle non-finite values.
Results may differ from a plain program's by a relative error of at most 0.011.
Values may be sent and summed in bfloat16 or wider, within the bound.
A program may use at most 64 MiB of HBM per device.

v0:
```python
import math

import jax
import jax.numpy as jnp
from jax import lax
from jax.sharding import PartitionSpec as P

STATIONS = 16
ROUNDS = 3


TWO_PI = 2.0 * math.pi
EPS = 1e-06


def swapped(block, axis, bit):
    count = lax.axis_size(axis)
    route = []
    for low in range(count):
        high = low | 1 << bit
        if high != low and high < count:
            route += [(low, high), (high, low)]
    return lax.ppermute(block, axis, route)


def forward_table(length):
    period = 2 * length
    times = jnp.arange(length, dtype=jnp.int32)[:, None]
    freqs = jnp.arange(period, dtype=jnp.int32)[None, :]
    angle = TWO_PI / period * (times * freqs % period).astype(jnp.float32)
    return jnp.concatenate([jnp.cos(angle), -jnp.sin(angle)], axis=1).astype(jnp.bfloat16)


def inverse_table(length, channels):
    period = 2 * length
    half = length // 2
    freqs = jnp.arange(period, dtype=jnp.int32)[:, None]
    lagged = jnp.arange(half, dtype=jnp.int32)[None, :] - half // 2
    angle = TWO_PI / period * (freqs * lagged % period).astype(jnp.float32)
    factor = 1.0 / (period * math.sqrt(channels * length))
    return (jnp.concatenate([jnp.cos(angle), -jnp.sin(angle)], axis=0) * factor).astype(
        jnp.bfloat16
    )


def spectra_of(block):
    events, stations, comps, length = block.shape
    traces = block.astype(jnp.float32)
    traces = traces - jnp.mean(traces, axis=-1, keepdims=True)
    traces = traces * lax.rsqrt(jnp.mean(traces * traces, axis=-1, keepdims=True) + EPS)
    traces = traces.astype(jnp.bfloat16).reshape(events * stations * comps, length)
    spec = jnp.dot(traces, forward_table(length), preferred_element_type=jnp.float32)
    return spec.astype(jnp.bfloat16).reshape(events, stations * comps, 4 * length)


def pair_curves(left, right, lag_table):
    slots, channels, width = left.shape
    period = width // 2
    left_real = left[:, :, :period]
    left_imag = left[:, :, period:]
    right_real = right[:, :, :period]
    right_imag = right[:, :, period:]
    real_part = jnp.einsum("pck,pck->pk", left_real, right_real, preferred_element_type=jnp.float32)
    real_part = real_part + jnp.einsum(
        "pck,pck->pk", left_imag, right_imag, preferred_element_type=jnp.float32
    )
    imag_part = jnp.einsum("pck,pck->pk", left_real, right_imag, preferred_element_type=jnp.float32)
    imag_part = imag_part - jnp.einsum(
        "pck,pck->pk", left_imag, right_real, preferred_element_type=jnp.float32
    )
    cross = jnp.concatenate([real_part, imag_part], axis=-1).astype(jnp.bfloat16)
    return jnp.dot(cross, lag_table, preferred_element_type=jnp.float32)


def fetch_waves(waveforms, bit_index):
    return swapped(waveforms, "region", bit_index)


def shards(waveforms, pair_lists, pair_counts):
    local_spec = spectra_of(waveforms)
    length = waveforms.shape[-1]
    lag_table = inverse_table(length, STATIONS * waveforms.shape[2])
    groups = lax.axis_size("station")
    share = pair_lists.shape[1] // groups
    sequence = list(range(ROUNDS))
    results = [None] * ROUNDS
    for round_index in sequence:
        partner_spec = spectra_of(fetch_waves(waveforms, round_index))
        slot_table = pair_lists[round_index]
        live_count = pair_counts[round_index, 0]

        def curve_term(
            start,
            count_rows,
            slot_table=slot_table,
            live_count=live_count,
            partner_spec=partner_spec,
        ):
            left = jnp.take(local_spec, slot_table[:, 0], axis=0)
            right = jnp.take(partner_spec, slot_table[:, 1], axis=0)
            curves = pair_curves(left, right, lag_table)
            live = jnp.arange(count_rows, dtype=jnp.int32) < live_count
            return jnp.where(live[:, None], curves, jnp.zeros_like(curves))

        results[round_index] = lax.psum_scatter(
            curve_term(jnp.int32(0), share * lax.axis_size("station")).astype(jnp.bfloat16),
            "station",
            scatter_dimension=0,
            tiled=True,
        ).astype(jnp.float32)
    return jnp.stack(results)


def solution(mesh):
    return jax.shard_map(
        shards,
        mesh=mesh,
        in_specs=(P("region", "station", None, None), P(None, "region", None), P(None, "region")),
        out_specs=P(None, ("region", "station"), None),
        check_vma=False,
    )
```

profile of v0, /device:TPU:1, one launch (start us, length us, event | category | flops | bytes accessed | tf_op | source)
XLA Modules:
  0.0 136.2 jit_solution(6304101311997231918)
XLA Ops:
  6.5 2.5 %collective-permute-start = (bf16[16,4,3,512]{3,1,2,0:T(4,128)(2,1)}, bf16[16,4,3,512]{3,1,2,0:T(4,128)(2,1)}, u32[]{:S(2)}, u32[]{:S(2)}) collective-permute-start(bf16[16,4,3,512]{3,1,2,0:T(4,128)(2,1)} %param.5), channel_id=1, source_target_pairs={{0,4},{4,0},{8,12},{12,8},{16,20},{20,16},{24,28},{28,24},{32,36},... | collective-permute-start | bytes 589832 | tf_op jit(solution)/shard_map/ppermute | solution.py:23
  9.0 3.0 %collective-permute-start.1 = (bf16[16,4,3,512]{3,1,2,0:T(4,128)(2,1)}, bf16[16,4,3,512]{3,1,2,0:T(4,128)(2,1)}, u32[]{:S(2)}, u32[]{:S(2)}) collective-permute-start(bf16[16,4,3,512]{3,1,2,0:T(4,128)(2,1)} %param.5), channel_id=1, source_target_pairs={{0,8},{8,0},{4,12},{12,4},{16,24},{24,16},{20,28},{28,20},{32,40},... | collective-permute-start | bytes 589832 | tf_op jit(solution)/shard_map/ppermute | solution.py:23
  12.0 4.2 %collective-permute-start.2 = (bf16[16,4,3,512]{3,1,2,0:T(4,128)(2,1)}, bf16[16,4,3,512]{3,1,2,0:T(4,128)(2,1)S(1)}, u32[]{:S(2)}, u32[]{:S(2)}) collective-permute-start(bf16[16,4,3,512]{3,1,2,0:T(4,128)(2,1)} %param.5), channel_id=1, source_target_pairs={{0,16},{16,0},{4,20},{20,4},{8,24},{24,8},{12,28},{28,12},{32,48},... | collective-permute-start | bytes 589832 | tf_op jit(solution)/shard_map/ppermute | solution.py:23
  16.2 8.5 %negate_convert_fusion = (bf16[512,1024]{1,0:T(8,128)(2,1)S(1)}, bf16[512,1024]{1,0:T(8,128)(2,1)S(1)}) fusion(), kind=kLoop, calls=%fused_computation.43 | loop fusion | flops 8912896 | bytes 2097152 | tf_op jit(solution)/shard_map/convert.11
  28.4 1.2 iota_compare_fusion.2
  30.8 2.0 %gather_fusion = bf16[32,12,2048]{2,1,0:T(8,128)(2,1)} fusion(bf16[16,12,2048]{2,1,0:T(8,128)(2,1)S(1)} %reshape.95, s32[1024]{0:T(1024)S(1)} %get-tuple-element.51), kind=kCustom, calls=%fused_computation.clone | custom fusion | bytes 3145856 | tf_op jit(solution)/shard_map/jit(_take)/gather | solution.py:99
  33.5 1.2 iota_compare_fusion.1
  34.7 2.0 %gather_fusion.4 = bf16[32,12,2048]{2,1,0:T(8,128)(2,1)} fusion(bf16[16,12,2048]{2,1,0:T(8,128)(2,1)S(1)} %reshape.95, s32[1024]{0:T(1024)S(1)} %pad_clamp_fusion.1), kind=kCustom, calls=%fused_computation.4.clone | custom fusion | bytes 3145856 | tf_op jit(solution)/shard_map/jit(_take)/gather | solution.py:99
  37.8 3.2 %broadcast_select_fusion.5 = bf16[32,12,2048]{2,1,0:T(8,128)(2,1)} fusion(bf16[32,12,2048]{2,1,0:T(8,128)(2,1)} %gather_fusion, pred[32]{0:T(512)(128)(4,1)S(1)} %copy-done.16), kind=kLoop, calls=%fused_computation.53 | loop fusion | flops 786432 | bytes 3145760 | tf_op jit(solution)/shard_map/jit(_take)/select_n | solution.py:99
  41.0 1.6 %broadcast_select_fusion.3 = bf16[32,12,2048]{2,1,0:T(8,128)(2,1)} fusion(bf16[32,12,2048]{2,1,0:T(8,128)(2,1)S(1)} %gather_fusion.2, pred[32]{0:T(512)(128)(4,1)S(1)} %get-tuple-element.46), kind=kLoop, calls=%fused_computation.51 | loop fusion | flops 786432 | bytes 3145760 | tf_op jit(solution)/shard_map/jit(_take)/select_n | solution.py:99
  44.0 5.1 %fusion.28 = (f32[1024,256]{1,0:T(8,128)}, f32[1024,256]{1,0:T(8,128)}) fusion(s32[256]{0:T(256)S(1)} %copy-done.17), kind=kLoop, calls=%fused_computation.82 | loop fusion | flops 3932160 | bytes 2098176 | tf_op jit(solution)/shard_map/cos | solution.py:41
  50.2 1.2 fusion.41
  51.4 1.1 fusion.42
  52.9 3.0 %convolution_convert_fusion.2 = bf16[192,2048]{1,0:T(8,128)(2,1)} fusion(bf16[192,512]{1,0:T(8,128)(2,1)S(1)} %reshape.96, bf16[512,1024]{1,0:T(8,128)(2,1)} %copy-done.4, bf16[512,1024]{1,0:T(8,128)(2,1)} %copy-done.5), kind=kOutput, calls=%fused_computation.23 | convolution fusion | flops 407240704 | bytes 3080192 | tf_op jit(solution)/shard_map/dot_general | solution.py:52
  55.9 1.3 reshape.97
  57.2 2.0 %gather_fusion.1 = bf16[32,12,2048]{2,1,0:T(8,128)(2,1)} fusion(bf16[16,12,2048]{2,1,0:T(8,128)(2,1)S(1)} %reshape.97, s32[1024]{0:T(1024)S(1)} %get-tuple-element.50), kind=kCustom, calls=%fused_computation.1.clone | custom fusion | bytes 3145856 | tf_op jit(solution)/shard_map/jit(_take)/gather | solution.py:100
  59.2 2.0 %broadcast_select_fusion.4 = bf16[32,12,2048]{2,1,0:T(8,128)(2,1)S(1)} fusion(bf16[32,12,2048]{2,1,0:T(8,128)(2,1)} %gather_fusion.1, pred[32]{0:T(512)(128)(4,1)S(1)} %copy-done.15), kind=kLoop, calls=%fused_computation.52 | loop fusion | flops 786432 | bytes 3145760 | tf_op jit(solution)/shard_map/jit(_take)/select_n | solution.py:100
  61.4 2.2 %fusion.2 = (f32[32,1024]{1,0:T(8,128)S(1)}, f32[32,1024]{1,0:T(8,128)S(1)}, f32[32,1024]{1,0:T(8,128)S(1)}, f32[32,1024]{1,0:T(8,128)S(1)}) fusion(bf16[32,12,2048]{2,1,0:T(8,128)(2,1)S(1)} %copy-done.1, bf16[32,12,2048]{2,1,0:T(8,128)(2,1)S(1)} %broadcast_select_fusion.4), kind=kLoop, calls=%fused_computation.27 | loop fusion | flops 4587520 | bytes 3670016 | tf_op jit(solution)/shard_map/pck,pck->pk/dot_general | solution.py:64
  65.9 1.2 fusion.39
  68.6 3.0 %convolution_convert_fusion.1 = bf16[192,2048]{1,0:T(8,128)(2,1)} fusion(bf16[192,512]{1,0:T(8,128)(2,1)S(1)} %reshape.98, bf16[512,1024]{1,0:T(8,128)(2,1)} %copy-done.4, bf16[512,1024]{1,0:T(8,128)(2,1)} %copy-done.5), kind=kOutput, calls=%fused_computation.22 | convolution fusion | flops 407240704 | bytes 3080192 | tf_op jit(solution)/shard_map/dot_general | solution.py:52
  71.6 1.3 reshape.99
  74.6 3.1 %convolution_convert_fusion = bf16[192,2048]{1,0:T(8,128)(2,1)} fusion(bf16[192,512]{1,0:T(8,128)(2,1)} %reshape.100, bf16[512,1024]{1,0:T(8,128)(2,1)} %copy-done.4, bf16[512,1024]{1,0:T(8,128)(2,1)} %copy-done.5), kind=kOutput, calls=%fused_computation.21 | convolution fusion | flops 407240704 | bytes 3080192 | tf_op jit(solution)/shard_map/dot_general | solution.py:52
  77.7 2.0 %gather_fusion.3 = bf16[32,12,2048]{2,1,0:T(8,128)(2,1)} fusion(bf16[16,12,2048]{2,1,0:T(8,128)(2,1)S(1)} %reshape.99, s32[1024]{0:T(1024)S(1)} %pad_clamp_fusion.2), kind=kCustom, calls=%fused_computation.3.clone | custom fusion | bytes 3145856 | tf_op jit(solution)/shard_map/jit(_take)/gather | solution.py:100
  79.7 2.0 %broadcast_select_fusion.2 = bf16[32,12,2048]{2,1,0:T(8,128)(2,1)S(1)} fusion(bf16[32,12,2048]{2,1,0:T(8,128)(2,1)} %gather_fusion.3, pred[32]{0:T(512)(128)(4,1)S(1)} %copy-done.14), kind=kLoop, calls=%fused_computation.50 | loop fusion | flops 786432 | bytes 3145760 | tf_op jit(solution)/shard_map/jit(_take)/select_n | solution.py:100
  81.9 2.2 %fusion.6 = (f32[32,1024]{1,0:T(8,128)S(1)}, f32[32,1024]{1,0:T(8,128)S(1)}, f32[32,1024]{1,0:T(8,128)S(1)}, f32[32,1024]{1,0:T(8,128)S(1)}) fusion(bf16[32,12,2048]{2,1,0:T(8,128)(2,1)S(1)} %copy-done, bf16[32,12,2048]{2,1,0:T(8,128)(2,1)S(1)} %broadcast_select_fusion.2), kind=kLoop, calls=%fused_computation.31 | loop fusion | flops 4587520 | bytes 3670016 | tf_op jit(solution)/shard_map/pck,pck->pk/dot_general | solution.py:64
  85.1 1.3 reshape.101
  86.4 2.0 %gather_fusion.5 = bf16[32,12,2048]{2,1,0:T(8,128)(2,1)} fusion(bf16[16,12,2048]{2,1,0:T(8,128)(2,1)S(1)} %reshape.101, s32[1024]{0:T(1024)S(1)} %pad_clamp_fusion), kind=kCustom, calls=%fused_computation.5.clone | custom fusion | bytes 3145856 | tf_op jit(solution)/shard_map/jit(_take)/gather | solution.py:100
  88.4 1.8 %broadcast_select_fusion = bf16[32,12,2048]{2,1,0:T(8,128)(2,1)S(1)} fusion(bf16[32,12,2048]{2,1,0:T(8,128)(2,1)} %gather_fusion.5, pred[32]{0:T(512)(128)(4,1)S(1)} %get-tuple-element.26), kind=kLoop, calls=%fused_computation.48 | loop fusion | flops 786432 | bytes 3145760 | tf_op jit(solution)/shard_map/jit(_take)/select_n | solution.py:100
  90.3 2.2 %fusion.10 = (f32[32,1024]{1,0:T(8,128)S(1)}, f32[32,1024]{1,0:T(8,128)S(1)}, f32[32,1024]{1,0:T(8,128)S(1)}, f32[32,1024]{1,0:T(8,128)S(1)}) fusion(bf16[32,12,2048]{2,1,0:T(8,128)(2,1)S(1)} %broadcast_select_fusion.1, bf16[32,12,2048]{2,1,0:T(8,128)(2,1)S(1)} %broadcast_select_fusion), kind=kLoop, calls=%fused_computation.35 | loop fusion | flops 4587520 | bytes 3670016 | tf_op jit(solution)/shard_map/pck,pck->pk/dot_general | solution.py:64
  93.5 12.2 %reduce-scatter.6.cloned.1.call-done = bf16[8,256]{1,0:T(8,128)(2,1)} async-done(((bf16[32,256]{1,0:T(8,128)(2,1)}), bf16[8,256]{1,0:T(8,128)(2,1)}) %reduce-scatter.6.cloned.1.call-update) | async-done | bytes 4112 | tf_op jit(solution)/shard_map/reduce_scatter | solution.py:105
  105.7 22.6 %reduce-scatter.8.cloned.1.call-done = bf16[8,256]{1,0:T(8,128)(2,1)} async-done(((bf16[32,256]{1,0:T(8,128)(2,1)}), bf16[8,256]{1,0:T(8,128)(2,1)}) %reduce-scatter.8.cloned.1.call-update) | async-done | bytes 4112 | tf_op jit(solution)/shard_map/reduce_scatter | solution.py:105
  128.4 1.3 maximum_convert_fusion
  (101 shorter events, 17.3 us)
Async XLA Ops:
  6.5 18.2 %copy-start.3 = (bf16[16,4,3,512]{3,1,2,0:T(4,128)(2,1)S(1)}, bf16[16,4,3,512]{3,1,2,0:T(4,128)(2,1)}, u32[]{:S(2)}) copy-start(bf16[16,4,3,512]{3,1,2,0:T(4,128)(2,1)} %param.5) | copy-start | bytes 589828
  6.5 19.1 %copy-start.13 = (s32[3,32,2]{1,2,0:T(2,128)S(1)}, s32[3,32,2]{1,2,0:T(2,128)}, u32[]{:S(2)}) copy-start(s32[3,32,2]{1,2,0:T(2,128)} %param.6) | copy-start | bytes 2308
  6.5 87.0 %reduce-scatter.4.cloned.1.call-start = ((), (), s32[]{:S(2)}) async-start(), calls=%async_computation.3 | async-start | bytes 20480 | tf_op jit(solution)/shard_map/reduce_scatter | solution.py:105
  6.5 42.5 %collective-permute-start = (bf16[16,4,3,512]{3,1,2,0:T(4,128)(2,1)}, bf16[16,4,3,512]{3,1,2,0:T(4,128)(2,1)}, u32[]{:S(2)}, u32[]{:S(2)}) collective-permute-start(bf16[16,4,3,512]{3,1,2,0:T(4,128)(2,1)} %param.5), channel_id=1, source_target_pairs={{0,4},{4,0},{8,12},{12,8},{16,20},{20,16},{24,28},{28,24},{32,36},... | collective-permute-start | bytes 589832 | tf_op jit(solution)/shard_map/ppermute | solution.py:23
  9.0 55.8 %collective-permute-start.1 = (bf16[16,4,3,512]{3,1,2,0:T(4,128)(2,1)}, bf16[16,4,3,512]{3,1,2,0:T(4,128)(2,1)}, u32[]{:S(2)}, u32[]{:S(2)}) collective-permute-start(bf16[16,4,3,512]{3,1,2,0:T(4,128)(2,1)} %param.5), channel_id=1, source_target_pairs={{0,8},{8,0},{4,12},{12,4},{16,24},{24,16},{20,28},{28,20},{32,40},... | collective-permute-start | bytes 589832 | tf_op jit(solution)/shard_map/ppermute | solution.py:23
  12.0 60.9 %collective-permute-start.2 = (bf16[16,4,3,512]{3,1,2,0:T(4,128)(2,1)}, bf16[16,4,3,512]{3,1,2,0:T(4,128)(2,1)S(1)}, u32[]{:S(2)}, u32[]{:S(2)}) collective-permute-start(bf16[16,4,3,512]{3,1,2,0:T(4,128)(2,1)} %param.5), channel_id=1, source_target_pairs={{0,16},{16,0},{4,20},{20,4},{8,24},{24,8},{12,28},{28,12},{32,48},... | collective-permute-start | bytes 589832 | tf_op jit(solution)/shard_map/ppermute | solution.py:23
  24.7 2.3 %copy-start.4 = (bf16[512,1024]{1,0:T(8,128)(2,1)}, bf16[512,1024]{1,0:T(8,128)(2,1)S(1)}, u32[]{:S(2)}) copy-start(bf16[512,1024]{1,0:T(8,128)(2,1)S(1)} %get-tuple-element.44) | copy-start | bytes 3145732
  24.7 2.9 %copy-start.5 = (bf16[512,1024]{1,0:T(8,128)(2,1)}, bf16[512,1024]{1,0:T(8,128)(2,1)S(1)}, u32[]{:S(2)}) copy-start(bf16[512,1024]{1,0:T(8,128)(2,1)S(1)} %get-tuple-element.45) | copy-start | bytes 3145732
  27.1 0.8 copy-start.12
  34.7 3.1 %copy-start.16 = (pred[32]{0:T(512)(128)(4,1)S(1)}, pred[32]{0:T(512)(128)(4,1)}, u32[]{:S(2)}) copy-start(pred[32]{0:T(512)(128)(4,1)} %get-tuple-element.33) | copy-start | bytes 100
  41.0 2.3 %copy-start.2 = (bf16[32,12,2048]{2,1,0:T(8,128)(2,1)S(1)}, bf16[32,12,2048]{2,1,0:T(8,128)(2,1)}, u32[]{:S(2)}) copy-start(bf16[32,12,2048]{2,1,0:T(8,128)(2,1)} %gather_fusion.4) | copy-start | bytes 4718596
  43.3 0.7 copy-start.17
  57.2 2.0 %copy-start.15 = (pred[32]{0:T(512)(128)(4,1)S(1)}, pred[32]{0:T(512)(128)(4,1)}, u32[]{:S(2)}) copy-start(pred[32]{0:T(512)(128)(4,1)} %get-tuple-element.18) | copy-start | bytes 100
  59.1 2.2 %copy-start.1 = (bf16[32,12,2048]{2,1,0:T(8,128)(2,1)S(1)}, bf16[32,12,2048]{2,1,0:T(8,128)(2,1)}, u32[]{:S(2)}) copy-start(bf16[32,12,2048]{2,1,0:T(8,128)(2,1)} %broadcast_select_fusion.5) | copy-start | bytes 4718596
  61.4 2.2 %copy-start.6 = (f32[1024,256]{1,0:T(8,128)S(1)}, f32[1024,256]{1,0:T(8,128)}, u32[]{:S(2)}) copy-start(f32[1024,256]{1,0:T(8,128)} %get-tuple-element.37) | copy-start | bytes 3145732
  61.4 2.3 %copy-start.9 = (f32[1024,256]{1,0:T(8,128)S(1)}, f32[1024,256]{1,0:T(8,128)}, u32[]{:S(2)}) copy-start(f32[1024,256]{1,0:T(8,128)} %get-tuple-element.38) | copy-start | bytes 3145732
  61.4 2.3 %copy-start.20 = (pred[32]{0:T(512)(128)(4,1)S(1)}, pred[32]{0:T(512)(128)(4,1)}, u32[]{:S(2)}) copy-start(pred[32]{0:T(512)(128)(4,1)} %iota_compare_fusion.2) | copy-start | bytes 100
  64.6 41.1 %reduce-scatter.6.cloned.1.call-start = ((), (), s32[]{:S(2)}) async-start(), calls=%async_computation.4 | async-start | bytes 20480 | tf_op jit(solution)/shard_map/reduce_scatter | solution.py:105
  77.7 2.0 %copy-start.14 = (pred[32]{0:T(512)(128)(4,1)S(1)}, pred[32]{0:T(512)(128)(4,1)}, u32[]{:S(2)}) copy-start(pred[32]{0:T(512)(128)(4,1)} %get-tuple-element.48) | copy-start | bytes 100
  79.7 2.2 %copy-start = (bf16[32,12,2048]{2,1,0:T(8,128)(2,1)S(1)}, bf16[32,12,2048]{2,1,0:T(8,128)(2,1)}, u32[]{:S(2)}) copy-start(bf16[32,12,2048]{2,1,0:T(8,128)(2,1)} %broadcast_select_fusion.3) | copy-start | bytes 4718596
  81.9 2.3 %copy-start.7 = (f32[1024,256]{1,0:T(8,128)S(1)}, f32[1024,256]{1,0:T(8,128)}, u32[]{:S(2)}) copy-start(f32[1024,256]{1,0:T(8,128)} %get-tuple-element.37) | copy-start | bytes 3145732
  81.9 2.3 %copy-start.10 = (f32[1024,256]{1,0:T(8,128)S(1)}, f32[1024,256]{1,0:T(8,128)}, u32[]{:S(2)}) copy-start(f32[1024,256]{1,0:T(8,128)} %get-tuple-element.38) | copy-start | bytes 3145732
  81.9 2.3 %copy-start.19 = (pred[32]{0:T(512)(128)(4,1)S(1)}, pred[32]{0:T(512)(128)(4,1)}, u32[]{:S(2)}) copy-start(pred[32]{0:T(512)(128)(4,1)} %iota_compare_fusion.1) | copy-start | bytes 100
  86.4 42.0 %reduce-scatter.8.cloned.1.call-start = ((), (), s32[]{:S(2)}) async-start(), calls=%async_computation.5 | async-start | bytes 20480 | tf_op jit(solution)/shard_map/reduce_scatter | solution.py:105
  90.3 2.2 %copy-start.8 = (f32[1024,256]{1,0:T(8,128)S(1)}, f32[1024,256]{1,0:T(8,128)}, u32[]{:S(2)}) copy-start(f32[1024,256]{1,0:T(8,128)} %get-tuple-element.37) | copy-start | bytes 3145732
  90.3 2.2 %copy-start.11 = (f32[1024,256]{1,0:T(8,128)S(1)}, f32[1024,256]{1,0:T(8,128)}, u32[]{:S(2)}) copy-start(f32[1024,256]{1,0:T(8,128)} %get-tuple-element.38) | copy-start | bytes 3145732
  90.3 2.2 %copy-start.18 = (pred[32]{0:T(512)(128)(4,1)S(1)}, pred[32]{0:T(512)(128)(4,1)}, u32[]{:S(2)}) copy-start(pred[32]{0:T(512)(128)(4,1)} %iota_compare_fusion) | copy-start | bytes 100
Sparse Core Ops, SparseCore 0:
  64.7 18.1 reduce-scatter.3
  86.5 19.1 reduce-scatter.5
  108.2 20.1 reduce-scatter.7
where the time goes:
time: 137 us; the launch traced here: 136 us
  other arithmetic  46.6 us (34%)
  waiting for transfers between devices  34.9 us (25%)
  local copies, waits for them, and re-layouts  18.7 us (14%)
  between operations  13.6 us (10%)
  matrix products  12.5 us (9%)
  starting transfers between devices  9.94 us (7%)
    reduce_scatter x3, waiting for transfers between devices, shards(): lax.psum_scatter(curve_term(jnp.int32(0), share * lax.axis_size('station'...  34.9 us
    dot_general x4, matrix products, spectra_of(): jnp.dot(traces, forward_table(length), preferred_element_type=jnp.float32)  9.79 us
    ppermute x3, starting transfers between devices, swapped(): return lax.ppermute(block, axis, route)  9.67 us
    another operation x7, other arithmetic  8.6 us
    dot_general x3, other arithmetic, pair_curves(): jnp.einsum('pck,pck->pk', left_imag, right_imag, preferred_element_type=j...  6.53 us
    gather x3, local copies, waits for them, and re-layouts, curve_term(): right = jnp.take(partner_spec, slot_table[:, 1], axis=0)  5.98 us
    select_n x3, other arithmetic, curve_term(): right = jnp.take(partner_spec, slot_table[:, 1], axis=0)  5.82 us
    cos x1, other arithmetic, inverse_table(): jnp.cos(angle)  5.1 us
  transfers between devices with their start and end apart: 6, of which 2 were waited for; matrix products, arithmetic and copies ran while one was open for 55% of the time, Pallas kernels for 0%

commit v1 on v0

v1 whole, which is shorter than its diff:
```python
import functools
import math

import jax
import jax.numpy as jnp
import numpy as np
from jax import lax
from jax.experimental import pallas as pl
from jax.experimental.pallas import tpu as pltpu
from jax.sharding import PartitionSpec as P

MESH = pl.DeviceIdType.MESH
ROUNDS = 3
EVENTS = 16
GROUP = 4
COMP = 3
LENGTH = 512
LAGS = 256
SLOTS = 32
STATIONS = 16
EPS = 1e-06
CHUNK = COMP * EVENTS
TRACES = GROUP * CHUNK
PERIOD = LENGTH + LAGS // 2
HALF = PERIOD // 2
WIDE = 3 * LAGS
LOWER = (2, 2, 3)


def tables():
    order = np.arange(HALF)
    times = np.arange(LENGTH)[:, None]
    angle = 2.0 * np.pi * ((2 * order[None, :] + 1) * times % (2 * PERIOD)) / (2 * PERIOD)
    real, imag = np.cos(angle), -np.sin(angle)
    forward = np.concatenate([real[:, :256], imag[:, :256], real[:, 256:], imag[:, 256:]], axis=1)
    lags = np.arange(LAGS)[None, :] - LAGS // 2
    angle = 2.0 * np.pi * ((2 * order[:, None] + 1) * lags % (2 * PERIOD)) / (2 * PERIOD)
    factor = 2.0 / (PERIOD * math.sqrt(STATIONS * COMP * LENGTH))
    cos, sin = factor * np.cos(angle), factor * np.sin(angle)
    inverse = np.concatenate(
        [cos[:256], -sin[:256], cos[256:], cos[256:], -sin[256:], sin[256:]], axis=0
    )
    return forward.astype(jnp.bfloat16), inverse.astype(jnp.bfloat16)


def kernel(
    x_hbm, lists_ref, forward_hbm, inverse_hbm, out_ref,
    x_in, forward, inverse, normal, arrived, spectra, theirs, left, right, total,
    message, heard, picks, shares, gathered,
    load_sem, wave_out, wave_in, list_out, list_in, share_out, share_in, ready,
):
    region, group = lax.axis_index("region"), lax.axis_index("station")
    z = lax.rem(region, 8)
    upper = [lax.rem(z // (1 << e), 2) for e in range(ROUNDS)]
    partner = [region + (1 << e) * (1 - 2 * upper[e]) for e in range(ROUNDS)]
    mates = [lax.rem(group + d, GROUP) for d in range(GROUP)]
    late = upper[2]

    barrier = pltpu.get_barrier_semaphore()

    def greet(which, to):
        pl.semaphore_signal(which, inc=1, device_id=to, device_id_type=MESH)

    for d in range(1, GROUP):
        greet(barrier, (region, mates[d]))
    for e in range(2):
        for d in range(GROUP):
            greet(barrier, (partner[e], mates[d]))

    @pl.when(late == 0)
    def _():
        for d in range(GROUP):
            greet(barrier, (partner[2], mates[d]))

    loads = [
        pltpu.make_async_copy(x_hbm, x_in, load_sem.at[0]),
        pltpu.make_async_copy(forward_hbm, forward, load_sem.at[1]),
        pltpu.make_async_copy(inverse_hbm, inverse, load_sem.at[2]),
    ]
    for load in loads:
        load.start()

    message[...] = jnp.zeros_like(message)
    for e in range(ROUNDS):
        message[2 * e : 2 * e + 2, 0:SLOTS] = lists_ref[e]
    mine = message[...]
    turned = pltpu.roll(mine, SLOTS, 1)
    even = lax.rem(lax.broadcasted_iota(jnp.int32, (8, 128), 0), 2) == 0
    turned = jnp.where(even, pltpu.roll(turned, 7, 0), pltpu.roll(turned, 1, 0))
    message[...] = turned

    loads[0].wait()
    traces = x_in[...].astype(jnp.float32).reshape(TRACES, LENGTH)
    traces = traces - jnp.mean(traces, axis=-1, keepdims=True)
    traces = traces * lax.rsqrt(jnp.mean(traces * traces, axis=-1, keepdims=True) + EPS)
    row = lax.broadcasted_iota(jnp.int32, (TRACES, TRACES), 0)
    column = lax.broadcasted_iota(jnp.int32, (TRACES, TRACES), 1)
    source = lax.rem(row, EVENTS) * (COMP * GROUP) + lax.rem(row // EVENTS, COMP) * GROUP + row // CHUNK
    reorder = jnp.where(column == source, 1.0, 0.0).astype(jnp.bfloat16)
    normal[...] = jnp.dot(
        reorder, traces.astype(jnp.bfloat16), preferred_element_type=jnp.float32
    ).astype(jnp.bfloat16)

    def rows(s):
        return pl.ds(pl.multiple_of(s * CHUNK, CHUNK), CHUNK)

    def wave(e, s):
        return pltpu.make_async_remote_copy(
            src_ref=normal.at[rows(s)],
            dst_ref=arrived.at[e, rows(s)],
            send_sem=wave_out.at[e, s],
            recv_sem=wave_in.at[e, s],
            device_id=(partner[e], group),
            device_id_type=MESH,
        )

    def listing(e):
        return pltpu.make_async_remote_copy(
            src_ref=message,
            dst_ref=heard.at[e],
            send_sem=list_out.at[e],
            recv_sem=list_in.at[e],
            device_id=(partner[e], group),
            device_id_type=MESH,
        )

    def share(e, side, d):
        to = region if side == 0 else partner[e]
        return pltpu.make_async_remote_copy(
            src_ref=shares.at[e, GROUP * side + mates[d]],
            dst_ref=gathered.at[e, GROUP * side + group],
            send_sem=share_out.at[e, GROUP * side + mates[d]],
            recv_sem=share_in.at[e, GROUP * side + group],
            device_id=(to, mates[d]),
            device_id_type=MESH,
        )

    def landed(e, side, d):
        to = region if side == 0 else partner[e]
        return pltpu.make_async_remote_copy(
            src_ref=shares.at[e, GROUP * side + mates[d]],
            dst_ref=gathered.at[e, GROUP * side + mates[d]],
            send_sem=share_out.at[e, GROUP * side + mates[d]],
            recv_sem=share_in.at[e, GROUP * side + mates[d]],
            device_id=(to, mates[d]),
            device_id_type=MESH,
        )

    first = [upper[e] * LOWER[e] for e in range(ROUNDS)]
    count = [LOWER[e] + upper[e] * (GROUP - 2 * LOWER[e]) for e in range(ROUNDS)]
    first_sent = [(1 - upper[e]) * LOWER[e] for e in range(ROUNDS)]

    def send(e):
        listing(e).start()

        @pl.loop(0, GROUP - count[e])
        def _(i):
            wave(e, first_sent[e] + i).start()

    @pl.when(late == 0)
    def _():
        pl.semaphore_wait(barrier, 11)

    @pl.when(late == 1)
    def _():
        pl.semaphore_wait(barrier, 15)
        for d in range(GROUP):
            greet(ready, (partner[2], mates[d]))
        send(2)

    send(0)
    send(1)

    loads[1].wait()
    spectra[...] = jnp.dot(
        normal[...], forward[...], preferred_element_type=jnp.float32
    ).astype(jnp.bfloat16)
    loads[2].wait()

    lane = lax.broadcasted_iota(jnp.int32, (8, 128), 1)
    cell = lax.broadcasted_iota(jnp.int32, (COMP * 2 * SLOTS, CHUNK), 1)
    part = lax.broadcasted_iota(jnp.int32, (COMP * 2 * SLOTS, CHUNK), 0) // (2 * SLOTS) * EVENTS
    theirs_row = lax.broadcasted_iota(jnp.int32, (2 * SLOTS, LAGS), 0) >= SLOTS

    for e in range(ROUNDS):
        if e == 1:

            @pl.when(late == 0)
            def _():
                pl.semaphore_wait(ready, GROUP)
                send(2)

        listing(e).wait_recv()
        events = jnp.where(lane < SLOTS, mine, heard[e]).astype(jnp.float32).T
        for side in range(2):
            event = events[: 2 * SLOTS, 2 * e + side : 2 * e + side + 1].astype(jnp.int32)
            event = jnp.concatenate([event] * COMP, axis=0)
            picks[side] = jnp.where(cell == part + event, 1.0, 0.0).astype(jnp.bfloat16)
        total[...] = jnp.zeros_like(total)

        @pl.loop(0, count[e])
        def _(i, e=e):
            s = first[e] + i
            wave(e, s).wait_recv()
            theirs[...] = jnp.dot(
                arrived[e, rows(s)], forward[...], preferred_element_type=jnp.float32
            ).astype(jnp.bfloat16)
            left[...] = jnp.dot(picks[0], spectra[rows(s)], preferred_element_type=jnp.float32)
            right[...] = jnp.dot(picks[1], theirs[...], preferred_element_type=jnp.float32)
            for c in range(COMP):
                at = pl.ds(c * 2 * SLOTS, 2 * SLOTS)
                lr, li, lm = left[at, 0:256], left[at, 256:512], left[at, 512:640]
                rr, ri, rm = right[at, 0:256], right[at, 256:512], right[at, 512:640]
                total[:, 0:256] += lr * rr + li * ri
                total[:, 256:512] += lr * ri - li * rr
                total[:, 512:640] += lm * rm
                total[:, 640:768] += lm * pltpu.roll(rm, 64, 1)

        real, imag, both, cross = total[:, 0:256], total[:, 256:512], total[:, 512:640], total[:, 640:768]
        imag = jnp.where(theirs_row, -imag, imag)
        cross = jnp.where(theirs_row[:, :128], -cross, cross)
        curves = jnp.dot(
            jnp.concatenate([real, imag, both, cross], axis=1).astype(jnp.bfloat16),
            inverse[...],
            preferred_element_type=jnp.float32,
        )
        for k in range(2 * GROUP):
            piece = curves[8 * k : 8 * k + 8]
            shares[e, k] = jnp.concatenate([piece[:, :128], piece[:, 128:]], axis=0).astype(jnp.bfloat16)
        for d in range(GROUP):
            share(e, 1, d).start()
        for d in range(1, GROUP):
            share(e, 0, d).start()
        gathered[e, pl.ds(group, 1)] = shares[e, pl.ds(group, 1)]

    for e in range(ROUNDS):
        for d in range(1, GROUP):
            landed(e, 0, d).wait_recv()
        for d in range(GROUP):
            landed(e, 1, d).wait_recv()
        curve = jnp.sum(gathered[e].astype(jnp.float32), axis=0)
        out_ref[e, :, 0:128] = curve[0:8]
        out_ref[e, :, 128:256] = curve[8:16]

    for e in range(ROUNDS):
        listing(e).wait_send()

        @pl.loop(0, GROUP - count[e])
        def _(i, e=e):
            wave(e, first_sent[e] + i).wait_send()

        for d in range(1, GROUP):
            share(e, 0, d).wait_send()
        for d in range(GROUP):
            share(e, 1, d).wait_send()


def shards(waveforms, pair_lists, pair_counts):
    forward, inverse = tables()
    bf16, f32 = jnp.bfloat16, jnp.float32
    dma = pltpu.SemaphoreType.DMA
    curves = pl.pallas_call(
        kernel,
        out_shape=jax.ShapeDtypeStruct((ROUNDS, 8, LAGS), f32),
        in_specs=[
            pl.BlockSpec(memory_space=pl.ANY),
            pl.BlockSpec(memory_space=pltpu.VMEM),
            pl.BlockSpec(memory_space=pl.ANY),
            pl.BlockSpec(memory_space=pl.ANY),
        ],
        out_specs=pl.BlockSpec(memory_space=pltpu.VMEM),
        scratch_shapes=[
            pltpu.VMEM((EVENTS, COMP, GROUP, LENGTH), bf16),
            pltpu.VMEM((LENGTH, PERIOD), bf16),
            pltpu.VMEM((WIDE, LAGS), bf16),
            pltpu.VMEM((TRACES, LENGTH), bf16),
            pltpu.VMEM((ROUNDS, TRACES, LENGTH), bf16),
            pltpu.VMEM((TRACES, PERIOD), bf16),
            pltpu.VMEM((CHUNK, PERIOD), bf16),
            pltpu.VMEM((COMP * 2 * SLOTS, PERIOD), f32),
            pltpu.VMEM((COMP * 2 * SLOTS, PERIOD), f32),
            pltpu.VMEM((2 * SLOTS, WIDE), f32),
            pltpu.VMEM((8, 128), jnp.int32),
            pltpu.VMEM((ROUNDS, 8, 128), jnp.int32),
            pltpu.VMEM((2, COMP * 2 * SLOTS, CHUNK), bf16),
            pltpu.VMEM((ROUNDS, 2 * GROUP, 16, 128), bf16),
            pltpu.VMEM((ROUNDS, 2 * GROUP, 16, 128), bf16),
            dma((3,)),
            dma((ROUNDS, GROUP)),
            dma((ROUNDS, GROUP)),
            dma((ROUNDS,)),
            dma((ROUNDS,)),
            dma((ROUNDS, 2 * GROUP)),
            dma((ROUNDS, 2 * GROUP)),
            pltpu.SemaphoreType.REGULAR,
        ],
        compiler_params=pltpu.CompilerParams(
            collective_id=0, has_side_effects=True, vmem_limit_bytes=48 * 2**20
        ),
        name="correlate",
    )(
        jnp.transpose(waveforms, (0, 2, 1, 3)),
        jnp.transpose(pair_lists, (0, 2, 1)),
        jnp.asarray(forward),
        jnp.asarray(inverse),
    )
    slot = lax.axis_index("station") * 8 + jnp.arange(8, dtype=jnp.int32)
    live = slot[None, :] < pair_counts
    return jnp.where(live[:, :, None], curves, jnp.zeros_like(curves))


def solution(mesh):
    return jax.shard_map(
        shards,
        mesh=mesh,
        in_specs=(P("region", "station", None, None), P(None, "region", None), P(None, "region")),
        out_specs=P(None, ("region", "station"), None),
        check_vma=False,
    )
```

time: 137 us -> 34.5 us (0.25)
  other arithmetic: 46.6 us -> 0.76 us
  waiting for transfers between devices: 34.9 us -> 0 us
  Pallas kernels: 0 us -> 29.2 us
  local copies, waits for them, and re-layouts: 18.7 us -> 4.27 us
  between operations: 13.6 us -> 0.02 us
  matrix products: 12.5 us -> 0 us
  starting transfers between devices: 9.94 us -> 0 us
    reduce_scatter x3 -> x0, waiting for transfers between devices: 34.9 us -> none  [shards(): lax.psum_scatter(curve_term(jnp.int32(0), share * lax.axis_size('station'...]
    pallas_call x0 -> x1, Pallas kernels: none -> 29.2 us  [shards(): pl.pallas_call(kernel, out_shape=jax.ShapeDtypeStruct((ROUNDS, 8, LAGS),...]
    dot_general x7 -> x0, matrix products: 12.5 us -> none  [the longest x4 9.79 us: spectra_of(): jnp.dot(traces, forward_table(length), preferred_element_type=jnp.float32)]
    gather x6 -> x0, local copies, waits for them, and re-layouts: 10.6 us -> none  [the longest x3 5.98 us: curve_term(): right = jnp.take(partner_spec, slot_table[:, 1], axis=0)]
    select_n x6 -> x1, other arithmetic: 10.9 us -> 0.68 us  [shards(): return jnp.where(live[:, :, None], curves, jnp.zeros_like(curves))]
    another operation x8 -> x0, other arithmetic: 9.93 us -> none
    ppermute x3 -> x0, starting transfers between devices: 9.67 us -> none  [swapped(): return lax.ppermute(block, axis, route)]
    dot_general x3 -> x0, other arithmetic: 6.53 us -> none  [pair_curves(): jnp.einsum('pck,pck->pk', left_imag, right_imag, preferred_element_type=j...]
  transfers between devices with their start and end apart: 6 -> 0, of which waited for: 2 -> 0; matrix products, arithmetic and copies ran while one was open for 55% -> 0% of each run, Pallas kernels for 0% -> 0%
where the time goes in v1:
time: 34.5 us; the launch traced here: 34.3 us
  Pallas kernels  29.2 us (85%)
  local copies, waits for them, and re-layouts  4.27 us (12%)
  other arithmetic  0.76 us (2%)
    pallas_call x1, Pallas kernels, shards(): pl.pallas_call(kernel, out_shape=jax.ShapeDtypeStruct((ROUNDS, 8, LAGS),...  29.2 us
    unnamed x10, local copies, waits for them, and re-layouts  4.27 us

profile of v1, /device:TPU:1, one launch (start us, length us, event | category | flops | bytes accessed | tf_op | source)
XLA Modules:
  0.0 34.3 jit_solution(9272908591555486569)
XLA Ops:
  0.0 0.0 copy-start.4
  0.0 0.7 %copy-done.4 = s32[3,1]{0,1:T(1,128)S(1)} copy-done((s32[3,1]{0,1:T(1,128)S(1)}, s32[3,1]{0,1:T(1,128)}, u32[]{:S(2)}) %copy-start.4) | copy-done | bytes 36
  0.7 0.0 copy-start.3
  0.7 0.1 broadcast_compare_fusion
  0.7 0.6 %copy-done.3 = s32[3,32,2]{1,2,0:T(2,128)S(1)} copy-done((s32[3,32,2]{1,2,0:T(2,128)S(1)}, s32[3,32,2]{1,2,0:T(2,128)}, u32[]{:S(2)}) %copy-start.3) | copy-done | bytes 792
  1.3 0.0 copy-start
  1.3 1.1 %copy-done = bf16[512,640]{1,0:T(8,128)(2,1)S(1)} copy-done((bf16[512,640]{1,0:T(8,128)(2,1)S(1)}, bf16[512,640]{1,0:T(8,128)(2,1)}, u32[]{:S(2)}) %copy-start) | copy-done | bytes 655384
  2.4 0.0 copy-start.1
  2.4 1.0 %copy-done.1 = bf16[768,256]{1,0:T(8,128)(2,1)S(1)} copy-done((bf16[768,256]{1,0:T(8,128)(2,1)S(1)}, bf16[768,256]{1,0:T(8,128)(2,1)}, u32[]{:S(2)}) %copy-start.1) | copy-done | bytes 393240
  3.4 0.0 copy-start.2
  3.4 0.9 %copy-done.2 = bf16[16,4,3,512]{3,1,2,0:T(4,128)(2,1)S(1)} copy-done((bf16[16,4,3,512]{3,1,2,0:T(4,128)(2,1)S(1)}, bf16[16,4,3,512]{3,1,2,0:T(4,128)(2,1)}, u32[]{:S(2)}) %copy-start.2) | copy-done | bytes 196632
  4.4 29.2 %correlate.1 = f32[3,8,256]{2,1,0:T(8,128)S(1)} custom-call(bf16[16,3,4,512]{3,2,1,0:T(4,128)(2,1)S(1)} %bitcast.3, s32[3,2,32]{2,1,0:T(2,128)S(1)} %bitcast.4, bf16[512,640]{1,0:T(8,128)(2,1)S(1)} %copy-done, bf16[768,256]{1,0:T(8,128)(2,1)S(1)} %copy-done.1), custom_call_target="tpu_custom_call" | custom-call | tf_op jit(solution)/shard_map/correlate/pallas_call | solution.py:262
  33.6 0.7 %broadcast_select_fusion = f32[3,8,256]{2,1,0:T(8,128)} fusion(f32[3,8,256]{2,1,0:T(8,128)S(1)} %correlate.1, pred[3,8]{1,0:T(4,128)(4,1)S(1)} %broadcast_compare_fusion), kind=kLoop, calls=%fused_computation | loop fusion | flops 6144 | bytes 49176 | tf_op jit(solution)/shard_map/jit(_where)/select_n | solution.py:309
  (1 shorter events, 0.0 us)
Async XLA Ops:
  0.0 0.7 %copy-start.4 = (s32[3,1]{0,1:T(1,128)S(1)}, s32[3,1]{0,1:T(1,128)}, u32[]{:S(2)}) copy-start(s32[3,1]{0,1:T(1,128)} %param.7) | copy-start | bytes 40
  0.7 0.7 %copy-start.3 = (s32[3,32,2]{1,2,0:T(2,128)S(1)}, s32[3,32,2]{1,2,0:T(2,128)}, u32[]{:S(2)}) copy-start(s32[3,32,2]{1,2,0:T(2,128)} %param.6) | copy-start | bytes 2308
  1.3 1.1 %copy-start = (bf16[512,640]{1,0:T(8,128)(2,1)S(1)}, bf16[512,640]{1,0:T(8,128)(2,1)}, u32[]{:S(2)}) copy-start(bf16[512,640]{1,0:T(8,128)(2,1)} %constant.12.clone.forward_hbm) | copy-start | bytes 1966084
  2.4 1.0 %copy-start.1 = (bf16[768,256]{1,0:T(8,128)(2,1)S(1)}, bf16[768,256]{1,0:T(8,128)(2,1)}, u32[]{:S(2)}) copy-start(bf16[768,256]{1,0:T(8,128)(2,1)} %constant.13.clone.inverse_hbm) | copy-start | bytes 1179652
  3.4 0.9 %copy-start.2 = (bf16[16,4,3,512]{3,1,2,0:T(4,128)(2,1)S(1)}, bf16[16,4,3,512]{3,1,2,0:T(4,128)(2,1)}, u32[]{:S(2)}) copy-start(bf16[16,4,3,512]{3,1,2,0:T(4,128)(2,1)} %param.5) | copy-start | bytes 589828

commit v2 on v1

--- a/solution.py
+++ b/solution.py
@@ -1,4 +1,3 @@
-import functools
 import math
 
 import jax
@@ -24,7 +23,8 @@
 PERIOD = LENGTH + LAGS // 2
 HALF = PERIOD // 2
 WIDE = 3 * LAGS
-LOWER = (2, 2, 3)
+GRANT = 60 * 2**20
+HALVES = 2
 
 
 def tables():
@@ -44,31 +44,41 @@
 
 
 def kernel(
-    x_hbm, lists_ref, forward_hbm, inverse_hbm, out_ref,
+    x_hbm, lists_ref, counts_ref, forward_hbm, inverse_hbm, out_ref,
     x_in, forward, inverse, normal, arrived, spectra, theirs, left, right, total,
     message, heard, picks, shares, gathered,
-    load_sem, wave_out, wave_in, list_out, list_in, share_out, share_in, ready,
+    load_sem, wave_out, wave_in, relay_out, list_out, list_in, share_out, share_in, near_ready, far_ready,
 ):
     region, group = lax.axis_index("region"), lax.axis_index("station")
     z = lax.rem(region, 8)
-    upper = [lax.rem(z // (1 << e), 2) for e in range(ROUNDS)]
-    partner = [region + (1 << e) * (1 - 2 * upper[e]) for e in range(ROUNDS)]
+    bits = [lax.rem(z // (1 << e), 2) for e in range(ROUNDS)]
+    step = [(1 << e) * (1 - 2 * bits[e]) for e in range(ROUNDS)]
+    partner = [region + step[e] for e in range(ROUNDS)]
+    onward = [region + step[0] + step[1], region + step[1] + step[2]]
     mates = [lax.rem(group + d, GROUP) for d in range(GROUP)]
-    late = upper[2]
+    late = bits[2]
+    middle = lax.rem(bits[0] + bits[1], 2)
+    odd = lax.rem(bits[0] + bits[1] + bits[2], 2)
+    worked, sent = odd * HALVES * CHUNK, (1 - odd) * HALVES * CHUNK
 
     barrier = pltpu.get_barrier_semaphore()
 
     def greet(which, to):
         pl.semaphore_signal(which, inc=1, device_id=to, device_id_type=MESH)
 
+    for e in range(2):
+        for d in range(GROUP):
+            greet(barrier, (partner[e], mates[d]))
     for d in range(1, GROUP):
         greet(barrier, (region, mates[d]))
-    for e in range(2):
-        for d in range(GROUP):
-            greet(barrier, (partner[e], mates[d]))
+
+    @pl.when(middle == 1)
+    def _():
+        greet(barrier, (onward[0], group))
 
     @pl.when(late == 0)
     def _():
+        greet(barrier, (onward[1], group))
         for d in range(GROUP):
             greet(barrier, (partner[2], mates[d]))
 
@@ -101,26 +111,36 @@
         reorder, traces.astype(jnp.bfloat16), preferred_element_type=jnp.float32
     ).astype(jnp.bfloat16)
 
-    def rows(s):
-        return pl.ds(pl.multiple_of(s * CHUNK, CHUNK), CHUNK)
-
-    def wave(e, s):
-        return pltpu.make_async_remote_copy(
-            src_ref=normal.at[rows(s)],
-            dst_ref=arrived.at[e, rows(s)],
-            send_sem=wave_out.at[e, s],
-            recv_sem=wave_in.at[e, s],
+    def rows(base, h):
+        return pl.ds(pl.multiple_of(base + h * CHUNK, CHUNK), CHUNK)
+
+    def wave(e, h):
+        return pltpu.make_async_remote_copy(
+            src_ref=normal.at[rows(sent, h)],
+            dst_ref=arrived.at[e, rows(0, h)],
+            send_sem=wave_out.at[e, h],
+            recv_sem=wave_in.at[e, h],
             device_id=(partner[e], group),
             device_id_type=MESH,
         )
 
+    def relay(e, h):
+        return pltpu.make_async_remote_copy(
+            src_ref=arrived.at[e, rows(0, h)],
+            dst_ref=arrived.at[e + 1, rows(0, h)],
+            send_sem=relay_out.at[e, h],
+            recv_sem=wave_in.at[e + 1, h],
+            device_id=(onward[e], group),
+            device_id_type=MESH,
+        )
+
     def listing(e):
         return pltpu.make_async_remote_copy(
-            src_ref=message,
+            src_ref=message if e < 2 else heard.at[1],
             dst_ref=heard.at[e],
             send_sem=list_out.at[e],
             recv_sem=list_in.at[e],
-            device_id=(partner[e], group),
+            device_id=(partner[e] if e < 2 else onward[1], group),
             device_id_type=MESH,
         )
 
@@ -146,34 +166,30 @@
             device_id_type=MESH,
         )
 
-    first = [upper[e] * LOWER[e] for e in range(ROUNDS)]
-    count = [LOWER[e] + upper[e] * (GROUP - 2 * LOWER[e]) for e in range(ROUNDS)]
-    first_sent = [(1 - upper[e]) * LOWER[e] for e in range(ROUNDS)]
-
-    def send(e):
-        listing(e).start()
-
-        @pl.loop(0, GROUP - count[e])
-        def _(i):
-            wave(e, first_sent[e] + i).start()
-
     @pl.when(late == 0)
     def _():
-        pl.semaphore_wait(barrier, 11)
+        pl.semaphore_wait(barrier, 11 + middle)
 
     @pl.when(late == 1)
     def _():
-        pl.semaphore_wait(barrier, 15)
-        for d in range(GROUP):
-            greet(ready, (partner[2], mates[d]))
-        send(2)
-
-    send(0)
-    send(1)
+        pl.semaphore_wait(barrier, 16 + middle)
+        greet(near_ready, (onward[1], group))
+        for d in range(GROUP):
+            greet(far_ready, (partner[2], mates[d]))
+
+    for h in range(HALVES):
+        wave(0, h).start()
+
+        @pl.when(middle == 1)
+        def _(h=h):
+            wave(1, h).start()
+
+    for e in range(2):
+        listing(e).start()
 
     loads[1].wait()
     spectra[...] = jnp.dot(
-        normal[...], forward[...], preferred_element_type=jnp.float32
+        normal[pl.ds(pl.multiple_of(worked, CHUNK), HALVES * CHUNK)], forward[...], preferred_element_type=jnp.float32
     ).astype(jnp.bfloat16)
     loads[2].wait()
 
@@ -182,15 +198,7 @@
     part = lax.broadcasted_iota(jnp.int32, (COMP * 2 * SLOTS, CHUNK), 0) // (2 * SLOTS) * EVENTS
     theirs_row = lax.broadcasted_iota(jnp.int32, (2 * SLOTS, LAGS), 0) >= SLOTS
 
-    for e in range(ROUNDS):
-        if e == 1:
-
-            @pl.when(late == 0)
-            def _():
-                pl.semaphore_wait(ready, GROUP)
-                send(2)
-
-        listing(e).wait_recv()
+    def work(e):
         events = jnp.where(lane < SLOTS, mine, heard[e]).astype(jnp.float32).T
         for side in range(2):
             event = events[: 2 * SLOTS, 2 * e + side : 2 * e + side + 1].astype(jnp.int32)
@@ -198,14 +206,14 @@
             picks[side] = jnp.where(cell == part + event, 1.0, 0.0).astype(jnp.bfloat16)
         total[...] = jnp.zeros_like(total)
 
-        @pl.loop(0, count[e])
-        def _(i, e=e):
-            s = first[e] + i
-            wave(e, s).wait_recv()
+        @pl.loop(0, HALVES)
+        def _(h):
+            if e == 2:
+                wave(e, h).wait_recv()
             theirs[...] = jnp.dot(
-                arrived[e, rows(s)], forward[...], preferred_element_type=jnp.float32
+                arrived[e, rows(0, h)], forward[...], preferred_element_type=jnp.float32
             ).astype(jnp.bfloat16)
-            left[...] = jnp.dot(picks[0], spectra[rows(s)], preferred_element_type=jnp.float32)
+            left[...] = jnp.dot(picks[0], spectra[rows(0, h)], preferred_element_type=jnp.float32)
             right[...] = jnp.dot(picks[1], theirs[...], preferred_element_type=jnp.float32)
             for c in range(COMP):
                 at = pl.ds(c * 2 * SLOTS, 2 * SLOTS)
@@ -227,28 +235,64 @@
         for k in range(2 * GROUP):
             piece = curves[8 * k : 8 * k + 8]
             shares[e, k] = jnp.concatenate([piece[:, :128], piece[:, 128:]], axis=0).astype(jnp.bfloat16)
+        if e == 2:
+
+            @pl.when(late == 0)
+            def _():
+                pl.semaphore_wait(far_ready, GROUP)
+
         for d in range(GROUP):
             share(e, 1, d).start()
         for d in range(1, GROUP):
             share(e, 0, d).start()
         gathered[e, pl.ds(group, 1)] = shares[e, pl.ds(group, 1)]
 
+    for h in range(HALVES):
+        wave(0, h).wait_recv()
+
+        @pl.when(middle == 1)
+        def _(h=h):
+            relay(0, h).start()
+
+    for h in range(HALVES):
+        wave(1, h).wait_recv()
+        if h == 0:
+
+            @pl.when(late == 0)
+            def _():
+                pl.semaphore_wait(near_ready, 1)
+
+        relay(1, h).start()
+    listing(1).wait_recv()
+    listing(2).start()
+    listing(0).wait_recv()
+    work(0)
+    work(1)
+    listing(2).wait_recv()
+    work(2)
+
+    slot = group * 8 + lax.rem(lax.broadcasted_iota(jnp.int32, (16, 128), 0), 8)
     for e in range(ROUNDS):
         for d in range(1, GROUP):
             landed(e, 0, d).wait_recv()
         for d in range(GROUP):
             landed(e, 1, d).wait_recv()
         curve = jnp.sum(gathered[e].astype(jnp.float32), axis=0)
+        curve = jnp.where(slot < counts_ref[0, e], curve, 0.0)
         out_ref[e, :, 0:128] = curve[0:8]
         out_ref[e, :, 128:256] = curve[8:16]
 
+    for h in range(HALVES):
+        wave(0, h).wait_send()
+        relay(1, h).wait_send()
+
+        @pl.when(middle == 1)
+        def _(h=h):
+            wave(1, h).wait_send()
+            relay(0, h).wait_send()
+
     for e in range(ROUNDS):
         listing(e).wait_send()
-
-        @pl.loop(0, GROUP - count[e])
-        def _(i, e=e):
-            wave(e, first_sent[e] + i).wait_send()
-
         for d in range(1, GROUP):
             share(e, 0, d).wait_send()
         for d in range(GROUP):
@@ -259,14 +303,15 @@
     forward, inverse = tables()
     bf16, f32 = jnp.bfloat16, jnp.float32
     dma = pltpu.SemaphoreType.DMA
-    curves = pl.pallas_call(
+    return pl.pallas_call(
         kernel,
         out_shape=jax.ShapeDtypeStruct((ROUNDS, 8, LAGS), f32),
         in_specs=[
-            pl.BlockSpec(memory_space=pl.ANY),
+            pl.BlockSpec(memory_space=pltpu.HBM),
             pl.BlockSpec(memory_space=pltpu.VMEM),
-            pl.BlockSpec(memory_space=pl.ANY),
-            pl.BlockSpec(memory_space=pl.ANY),
+            pl.BlockSpec(memory_space=pltpu.SMEM),
+            pl.BlockSpec(memory_space=pltpu.HBM),
+            pl.BlockSpec(memory_space=pltpu.HBM),
         ],
         out_specs=pl.BlockSpec(memory_space=pltpu.VMEM),
         scratch_shapes=[
@@ -274,8 +319,8 @@
             pltpu.VMEM((LENGTH, PERIOD), bf16),
             pltpu.VMEM((WIDE, LAGS), bf16),
             pltpu.VMEM((TRACES, LENGTH), bf16),
-            pltpu.VMEM((ROUNDS, TRACES, LENGTH), bf16),
-            pltpu.VMEM((TRACES, PERIOD), bf16),
+            pltpu.VMEM((ROUNDS, HALVES * CHUNK, LENGTH), bf16),
+            pltpu.VMEM((HALVES * CHUNK, PERIOD), bf16),
             pltpu.VMEM((CHUNK, PERIOD), bf16),
             pltpu.VMEM((COMP * 2 * SLOTS, PERIOD), f32),
             pltpu.VMEM((COMP * 2 * SLOTS, PERIOD), f32),
@@ -286,27 +331,27 @@
             pltpu.VMEM((ROUNDS, 2 * GROUP, 16, 128), bf16),
             pltpu.VMEM((ROUNDS, 2 * GROUP, 16, 128), bf16),
             dma((3,)),
-            dma((ROUNDS, GROUP)),
-            dma((ROUNDS, GROUP)),
+            dma((2, HALVES)),
+            dma((ROUNDS, HALVES)),
+            dma((2, HALVES)),
             dma((ROUNDS,)),
             dma((ROUNDS,)),
             dma((ROUNDS, 2 * GROUP)),
             dma((ROUNDS, 2 * GROUP)),
             pltpu.SemaphoreType.REGULAR,
+            pltpu.SemaphoreType.REGULAR,
         ],
         compiler_params=pltpu.CompilerParams(
-            collective_id=0, has_side_effects=True, vmem_limit_bytes=48 * 2**20
+            collective_id=0, has_side_effects=True, vmem_limit_bytes=GRANT
         ),
         name="correlate",
     )(
         jnp.transpose(waveforms, (0, 2, 1, 3)),
         jnp.transpose(pair_lists, (0, 2, 1)),
+        jnp.transpose(pair_counts, (1, 0)),
         jnp.asarray(forward),
         jnp.asarray(inverse),
     )
-    slot = lax.axis_index("station") * 8 + jnp.arange(8, dtype=jnp.int32)
-    live = slot[None, :] < pair_counts
-    return jnp.where(live[:, :, None], curves, jnp.zeros_like(curves))
 
 
 def solution(mesh):

time: 34.5 us -> 26.7 us (0.77)
  Pallas kernels: 29.2 us -> 25.2 us
  local copies, waits for them, and re-layouts: 4.27 us -> 1.35 us
  other arithmetic: 0.76 us -> 0 us
    pallas_call x1, Pallas kernels: 29.2 us -> 25.2 us  [shards(): pl.pallas_call(kernel, out_shape=jax.ShapeDtypeStruct((ROUNDS, 8, LAGS),...]
    unnamed x10 -> x1, local copies, waits for them, and re-layouts: 4.27 us -> 1.35 us
    select_n x1 -> x0, other arithmetic: 0.68 us -> none  [shards(): return jnp.where(live[:, :, None], curves, jnp.zeros_like(curves))]
where the time goes in v2:
time: 26.7 us; the launch traced here: 26.5 us
  Pallas kernels  25.2 us (94%)
  local copies, waits for them, and re-layouts  1.35 us (5%)
    pallas_call x1, Pallas kernels, shards(): pl.pallas_call(kernel, out_shape=jax.ShapeDtypeStruct((ROUNDS, 8, LAGS),...  25.2 us
    unnamed x1, local copies, waits for them, and re-layouts  1.35 us

profile of v2, /device:TPU:1, one launch (start us, length us, event | category | flops | bytes accessed | tf_op | source)
XLA Modules:
  0.0 26.5 jit_solution(10394709756077214867)
XLA Ops:
  0.0 25.2 %correlate.1 = f32[3,8,256]{2,1,0:T(8,128)} custom-call(bf16[16,3,4,512]{3,2,1,0:T(4,128)(2,1)} %bitcast.3, s32[3,2,32]{2,1,0:T(2,128)} %bitcast.4, s32[1,3]{1,0:T(1,128)} %bitcast.5, bf16[512,640]{1,0:T(8,128)(2,1)} %constant.4.clone.forward_hbm, bf16[768,256]{1,0:T(8,128)(2,1)} %constant.5.clone.inverse_hbm), custom_call_target="tpu_custom_call" | custom-call | tf_op jit(solution)/shard_map/correlate/pallas_call | solution.py:306
  25.2 1.3 %copy.7 = f32[3,8,256]{2,1,0:T(8,128)} copy(f32[3,8,256]{2,1,0:T(8,128)} %correlate.1) | data formatting | bytes 49152

commit v3 on v1

v3 whole, which is shorter than its diff:
```python
import math

import jax
import jax.numpy as jnp
import numpy as np
from jax import lax
from jax.experimental import pallas as pl
from jax.experimental.pallas import tpu as pltpu
from jax.sharding import PartitionSpec as P

MESH = pl.DeviceIdType.MESH
ROUNDS = 3
EVENTS = 16
GROUP = 4
COMP = 3
LENGTH = 512
LAGS = 256
SLOTS = 32
STATIONS = 16
EPS = 1e-06
CHUNK = COMP * EVENTS
TRACES = GROUP * CHUNK
PERIOD = LENGTH + LAGS // 2
HALF = PERIOD // 2
WIDE = 3 * LAGS
GRANT = 55200 * 2**10
HALVES = 2


def tables():
    order = np.arange(HALF)
    times = np.arange(LENGTH)[:, None]
    angle = 2.0 * np.pi * ((2 * order[None, :] + 1) * times % (2 * PERIOD)) / (2 * PERIOD)
    real, imag = np.cos(angle), -np.sin(angle)
    forward = np.concatenate([real[:, :256], imag[:, :256], real[:, 256:], imag[:, 256:]], axis=1)
    lags = np.arange(LAGS)[None, :] - LAGS // 2
    angle = 2.0 * np.pi * ((2 * order[:, None] + 1) * lags % (2 * PERIOD)) / (2 * PERIOD)
    factor = 2.0 / (PERIOD * math.sqrt(STATIONS * COMP * LENGTH))
    cos, sin = factor * np.cos(angle), factor * np.sin(angle)
    inverse = np.concatenate(
        [cos[:256], -sin[:256], cos[256:], cos[256:], -sin[256:], sin[256:]], axis=0
    )
    return forward.astype(jnp.bfloat16), inverse.astype(jnp.bfloat16)


def kernel(
    x_hbm, lists_hbm, counts_hbm, forward_hbm, inverse_hbm, out_ref,
    x_in, lists_ref, counts_ref, forward, inverse, normal, arrived, spectra, left, right, total,
    message, heard, picks, shares, gathered,
    load_sem, wave_out, wave_in, list_out, list_in, share_out, share_in, ready, settled,
):
    region, group = lax.axis_index("region"), lax.axis_index("station")
    z = lax.rem(region, 8)
    bits = [lax.rem(z // (1 << e), 2) for e in range(ROUNDS)]
    step = [(1 << e) * (1 - 2 * bits[e]) for e in range(ROUNDS)]
    partner = [region + step[0], region + step[1], region + step[1] + step[2]]
    mates = [lax.rem(group + d, GROUP) for d in range(GROUP)]
    late = bits[2]
    odd = lax.rem(bits[0] + bits[1] + bits[2], 2)
    worked, sent = odd * HALVES * CHUNK, (1 - odd) * HALVES * CHUNK

    barrier = pltpu.get_barrier_semaphore()

    def greet(which, to):
        pl.semaphore_signal(which, inc=1, device_id=to, device_id_type=MESH)

    greet(barrier, (partner[1], group))
    greet(barrier, (partner[0], group))
    for d in range(1, GROUP):
        greet(barrier, (region, mates[d]))

    @pl.when(late == 0)
    def _():
        greet(barrier, (partner[2], group))

    loads = [
        pltpu.make_async_copy(x_hbm, x_in, load_sem.at[0]),
        pltpu.make_async_copy(forward_hbm, forward, load_sem.at[1]),
        pltpu.make_async_copy(inverse_hbm, inverse, load_sem.at[2]),
        pltpu.make_async_copy(lists_hbm, lists_ref, load_sem.at[3]),
        pltpu.make_async_copy(counts_hbm, counts_ref, load_sem.at[4]),
    ]
    for load in loads:
        load.start()

    loads[3].wait()
    message[...] = jnp.zeros_like(message)
    for e in range(ROUNDS):
        message[2 * e : 2 * e + 2, 0:SLOTS] = lists_ref[e]
    mine = message[...]
    turned = pltpu.roll(mine, SLOTS, 1)
    even = lax.rem(lax.broadcasted_iota(jnp.int32, (8, 128), 0), 2) == 0
    turned = jnp.where(even, pltpu.roll(turned, 7, 0), pltpu.roll(turned, 1, 0))
    message[...] = mine + turned

    loads[0].wait()
    traces = x_in[...].astype(jnp.float32).reshape(TRACES, LENGTH)
    traces = traces - jnp.mean(traces, axis=-1, keepdims=True)
    traces = traces * lax.rsqrt(jnp.mean(traces * traces, axis=-1, keepdims=True) + EPS)
    row = lax.broadcasted_iota(jnp.int32, (TRACES, TRACES), 0)
    column = lax.broadcasted_iota(jnp.int32, (TRACES, TRACES), 1)
    source = lax.rem(row, EVENTS) * (COMP * GROUP) + lax.rem(row // EVENTS, COMP) * GROUP + row // CHUNK
    reorder = jnp.where(column == source, 1.0, 0.0).astype(jnp.bfloat16)
    normal[...] = jnp.dot(
        reorder, traces.astype(jnp.bfloat16), preferred_element_type=jnp.float32
    ).astype(jnp.bfloat16)

    def rows(base, h):
        return pl.ds(pl.multiple_of(base + h * CHUNK, CHUNK), CHUNK)

    def wave(e, h):
        return pltpu.make_async_remote_copy(
            src_ref=normal.at[rows(sent if e < 2 else worked, h)],
            dst_ref=arrived.at[e, rows(0, h)],
            send_sem=wave_out.at[e, h],
            recv_sem=wave_in.at[e, h],
            device_id=(partner[e], group),
            device_id_type=MESH,
        )

    def listing(e):
        return pltpu.make_async_remote_copy(
            src_ref=message,
            dst_ref=heard.at[e],
            send_sem=list_out.at[e],
            recv_sem=list_in.at[e],
            device_id=(partner[e], group),
            device_id_type=MESH,
        )

    def share(e, side, d):
        to = partner[e] if side == 1 else partner[1] if e == 2 else region
        return pltpu.make_async_remote_copy(
            src_ref=shares.at[e, GROUP * side + mates[d]],
            dst_ref=gathered.at[e, GROUP * side + group],
            send_sem=share_out.at[e, GROUP * side + mates[d]],
            recv_sem=share_in.at[e, GROUP * side + group],
            device_id=(to, mates[d]),
            device_id_type=MESH,
        )

    def landed(e, side, d):
        to = partner[e] if side == 1 else partner[1] if e == 2 else region
        return pltpu.make_async_remote_copy(
            src_ref=shares.at[e, GROUP * side + mates[d]],
            dst_ref=gathered.at[e, GROUP * side + mates[d]],
            send_sem=share_out.at[e, GROUP * side + mates[d]],
            recv_sem=share_in.at[e, GROUP * side + mates[d]],
            device_id=(to, mates[d]),
            device_id_type=MESH,
        )

    def send(e):
        for h in range(HALVES):
            wave(e, h).start()
        listing(e).start()

    @pl.when(late == 0)
    def _():
        pl.semaphore_wait(barrier, 5)

    @pl.when(late == 1)
    def _():
        pl.semaphore_wait(barrier, 6)
        greet(ready, (partner[2], group))
        send(2)

    send(1)
    send(0)

    loads[1].wait()
    spectra[0] = jnp.dot(
        normal[pl.ds(pl.multiple_of(worked, CHUNK), HALVES * CHUNK)], forward[...], preferred_element_type=jnp.float32
    ).astype(jnp.bfloat16)
    loads[2].wait()
    loads[4].wait()

    @pl.when(late == 0)
    def _():
        pl.semaphore_wait(ready, 1)
        send(2)

    for d in range(1, GROUP):
        greet(settled, (region, mates[d]))

    lane = lax.broadcasted_iota(jnp.int32, (8, 128), 1)
    cell = lax.broadcasted_iota(jnp.int32, (COMP * 2 * SLOTS, CHUNK), 1)
    part = lax.broadcasted_iota(jnp.int32, (COMP * 2 * SLOTS, CHUNK), 0) // (2 * SLOTS) * EVENTS
    theirs_row = lax.broadcasted_iota(jnp.int32, (2 * SLOTS, LAGS), 0) >= SLOTS

    def work(e):
        listing(e).wait_recv()
        events = jnp.where(lane < SLOTS, heard[1] if e == 2 else message[...], heard[e]).astype(jnp.float32).T
        for side in range(2):
            event = events[: 2 * SLOTS, 2 * e + side : 2 * e + side + 1].astype(jnp.int32)
            event = jnp.concatenate([event] * COMP, axis=0)
            picks[side] = jnp.where(cell == part + event, 1.0, 0.0).astype(jnp.bfloat16)
        total[...] = jnp.zeros_like(total)

        @pl.loop(0, HALVES)
        def _(h):
            wave(e, h).wait_recv()
            spectra[1 + e, rows(0, h)] = jnp.dot(
                arrived[e, rows(0, h)], forward[...], preferred_element_type=jnp.float32
            ).astype(jnp.bfloat16)
            left[...] = jnp.dot(picks[0], spectra[e if e == 2 else 0, rows(0, h)], preferred_element_type=jnp.float32)
            right[...] = jnp.dot(picks[1], spectra[1 + e, rows(0, h)], preferred_element_type=jnp.float32)
            for c in range(COMP):
                at = pl.ds(c * 2 * SLOTS, 2 * SLOTS)
                lr, li, lm = left[at, 0:256], left[at, 256:512], left[at, 512:640]
                rr, ri, rm = right[at, 0:256], right[at, 256:512], right[at, 512:640]
                total[:, 0:256] += lr * rr + li * ri
                total[:, 256:512] += lr * ri - li * rr
                total[:, 512:640] += lm * rm
                total[:, 640:768] += lm * pltpu.roll(rm, 64, 1)

        real, imag, both, cross = total[:, 0:256], total[:, 256:512], total[:, 512:640], total[:, 640:768]
        imag = jnp.where(theirs_row, -imag, imag)
        cross = jnp.where(theirs_row[:, :128], -cross, cross)
        curves = jnp.dot(
            jnp.concatenate([real, imag, both, cross], axis=1).astype(jnp.bfloat16),
            inverse[...],
            preferred_element_type=jnp.float32,
        )
        for k in range(2 * GROUP):
            piece = curves[8 * k : 8 * k + 8]
            shares[e, k] = jnp.concatenate([piece[:, :128], piece[:, 128:]], axis=0).astype(jnp.bfloat16)
        for side in range(2):
            for d in range(GROUP):
                if e == 2 or side == 1 or d > 0:
                    share(e, side, d).start()
        if e < 2:
            gathered[e, pl.ds(group, 1)] = shares[e, pl.ds(group, 1)]

    pl.semaphore_wait(settled, GROUP - 1)
    work(1)

    @pl.when(late == 0)
    def _():
        work(0)

    work(2)

    @pl.when(late == 1)
    def _():
        work(0)

    slot = group * 8 + lax.rem(lax.broadcasted_iota(jnp.int32, (16, 128), 0), 8)
    for e in range(ROUNDS):
        for side in range(2):
            for d in range(GROUP):
                if e == 2 or side == 1 or d > 0:
                    landed(e, side, d).wait_recv()
        curve = jnp.sum(gathered[e].astype(jnp.float32), axis=0)
        curve = jnp.where(slot < counts_ref[0, e], curve, 0.0)
        out_ref[e, :, 0:128] = curve[0:8]
        out_ref[e, :, 128:256] = curve[8:16]

    for e in range(ROUNDS):
        listing(e).wait_send()
        for h in range(HALVES):
            wave(e, h).wait_send()
        for side in range(2):
            for d in range(GROUP):
                if e == 2 or side == 1 or d > 0:
                    share(e, side, d).wait_send()


def shards(waveforms, pair_lists, pair_counts):
    forward, inverse = tables()
    bf16, f32 = jnp.bfloat16, jnp.float32
    dma = pltpu.SemaphoreType.DMA
    return pl.pallas_call(
        kernel,
        out_shape=jax.ShapeDtypeStruct((ROUNDS, 8, LAGS), f32),
        in_specs=[
            pl.BlockSpec(memory_space=pl.ANY),
            pl.BlockSpec(memory_space=pl.ANY),
            pl.BlockSpec(memory_space=pl.ANY),
            pl.BlockSpec(memory_space=pl.ANY),
            pl.BlockSpec(memory_space=pl.ANY),
        ],
        out_specs=pl.BlockSpec(memory_space=pltpu.VMEM),
        scratch_shapes=[
            pltpu.VMEM((EVENTS, COMP, GROUP, LENGTH), bf16),
            pltpu.VMEM((ROUNDS, 2, SLOTS), jnp.int32),
            pltpu.SMEM((1, ROUNDS), jnp.int32),
            pltpu.VMEM((LENGTH, PERIOD), bf16),
            pltpu.VMEM((WIDE, LAGS), bf16),
            pltpu.VMEM((TRACES, LENGTH), bf16),
            pltpu.VMEM((ROUNDS, HALVES * CHUNK, LENGTH), bf16),
            pltpu.VMEM((1 + ROUNDS, HALVES * CHUNK, PERIOD), bf16),
            pltpu.VMEM((COMP * 2 * SLOTS, PERIOD), f32),
            pltpu.VMEM((COMP * 2 * SLOTS, PERIOD), f32),
            pltpu.VMEM((2 * SLOTS, WIDE), f32),
            pltpu.VMEM((8, 128), jnp.int32),
            pltpu.VMEM((ROUNDS, 8, 128), jnp.int32),
            pltpu.VMEM((2, COMP * 2 * SLOTS, CHUNK), bf16),
            pltpu.VMEM((ROUNDS, 2 * GROUP, 16, 128), bf16),
            pltpu.VMEM((ROUNDS, 2 * GROUP, 16, 128), bf16),
            dma((5,)),
            dma((ROUNDS, HALVES)),
            dma((ROUNDS, HALVES)),
            dma((ROUNDS,)),
            dma((ROUNDS,)),
            dma((ROUNDS, 2 * GROUP)),
            dma((ROUNDS, 2 * GROUP)),
            pltpu.SemaphoreType.REGULAR,
            pltpu.SemaphoreType.REGULAR,
        ],
        compiler_params=pltpu.CompilerParams(
            collective_id=0, has_side_effects=True, vmem_limit_bytes=GRANT
        ),
        name="correlate",
    )(
        jnp.transpose(waveforms, (0, 2, 1, 3)),
        jnp.transpose(pair_lists, (0, 2, 1)),
        jnp.transpose(pair_counts, (1, 0)),
        jnp.asarray(forward),
        jnp.asarray(inverse),
    )


def solution(mesh):
    return jax.shard_map(
        shards,
        mesh=mesh,
        in_specs=(P("region", "station", None, None), P(None, "region", None), P(None, "region")),
        out_specs=P(None, ("region", "station"), None),
        check_vma=False,
    )
```

time: 34.5 us -> 23.9 us (0.69)
  Pallas kernels: 29.2 us -> 22.5 us
  local copies, waits for them, and re-layouts: 4.27 us -> 1.3 us
  other arithmetic: 0.76 us -> 0 us
    pallas_call x1, Pallas kernels: 29.2 us -> 22.5 us  [shards(): pl.pallas_call(kernel, out_shape=jax.ShapeDtypeStruct((ROUNDS, 8, LAGS),...]
    unnamed x10 -> x5, local copies, waits for them, and re-layouts: 4.27 us -> 1.3 us
    select_n x1 -> x0, other arithmetic: 0.68 us -> none  [shards(): return jnp.where(live[:, :, None], curves, jnp.zeros_like(curves))]
where the time goes in v3:
time: 23.9 us; the launch traced here: 23.8 us
  Pallas kernels  22.5 us (94%)
  local copies, waits for them, and re-layouts  1.3 us (5%)
    pallas_call x1, Pallas kernels, shards(): pl.pallas_call(kernel, out_shape=jax.ShapeDtypeStruct((ROUNDS, 8, LAGS),...  22.5 us
    unnamed x5, local copies, waits for them, and re-layouts  1.3 us

profile of v3, /device:TPU:1, one launch (start us, length us, event | category | flops | bytes accessed | tf_op | source)
XLA Modules:
  0.0 23.8 jit_solution(15896919086973061537)
XLA Ops:
  0.0 0.0 copy-start
  0.0 0.0 copy-start.1
  0.0 0.7 %copy-done = s32[3,32,2]{1,2,0:T(2,128)S(1)} copy-done((s32[3,32,2]{1,2,0:T(2,128)S(1)}, s32[3,32,2]{1,2,0:T(2,128)}, u32[]{:S(2)}) %copy-start) | copy-done | bytes 792
  0.7 0.0 copy-done.1
  0.7 22.5 %correlate.1 = f32[3,8,256]{2,1,0:T(8,128)S(1)} custom-call(bf16[16,3,4,512]{3,2,1,0:T(4,128)(2,1)} %bitcast.5, s32[3,2,32]{2,1,0:T(2,128)S(1)} %bitcast.3, s32[1,3]{1,0:T(1,128)S(1)} %bitcast.4, bf16[512,640]{1,0:T(8,128)(2,1)} %constant.4.clone.forward_hbm, bf16[768,256]{1,0:T(8,128)(2,1)} %constant.5.clone.inverse_hbm), custom_call_target="tpu_custom_call" | custom-call | tf_op jit(solution)/shard_map/correlate/pallas_call | solution.py:273
  23.2 0.6 %copy.7 = f32[3,8,256]{2,1,0:T(8,128)} copy(f32[3,8,256]{2,1,0:T(8,128)S(1)} %correlate.1) | data formatting | bytes 49152
Async XLA Ops:
  0.0 0.7 %copy-start = (s32[3,32,2]{1,2,0:T(2,128)S(1)}, s32[3,32,2]{1,2,0:T(2,128)}, u32[]{:S(2)}) copy-start(s32[3,32,2]{1,2,0:T(2,128)} %param.6) | copy-start | bytes 2308
  0.0 0.7 %copy-start.1 = (s32[3,1]{0,1:T(1,128)S(1)}, s32[3,1]{0,1:T(1,128)}, u32[]{:S(2)}) copy-start(s32[3,1]{0,1:T(1,128)} %param.7) | copy-start | bytes 40

commit v4 on v3

--- a/solution.py
+++ b/solution.py
@@ -25,6 +25,8 @@
 WIDE = 3 * LAGS
 GRANT = 55200 * 2**10
 HALVES = 2
+SHIFT = 2
+LEFT_OUT = SHIFT * EVENTS
 
 
 def tables():
@@ -59,6 +61,8 @@
     odd = lax.rem(bits[0] + bits[1] + bits[2], 2)
     worked, sent = odd * HALVES * CHUNK, (1 - odd) * HALVES * CHUNK
 
+    arrived[1, HALVES * CHUNK :] = jnp.zeros_like(arrived[1, HALVES * CHUNK :])
+    arrived[2, HALVES * CHUNK - LEFT_OUT :] = jnp.zeros_like(arrived[2, HALVES * CHUNK - LEFT_OUT :])
     barrier = pltpu.get_barrier_semaphore()
 
     def greet(which, to):
@@ -108,15 +112,30 @@
     def rows(base, h):
         return pl.ds(pl.multiple_of(base + h * CHUNK, CHUNK), CHUNK)
 
-    def wave(e, h):
+    def copy(e, h, src, dst, size):
         return pltpu.make_async_remote_copy(
-            src_ref=normal.at[rows(sent if e < 2 else worked, h)],
-            dst_ref=arrived.at[e, rows(0, h)],
+            src_ref=normal.at[pl.ds(pl.multiple_of(src, EVENTS), size)],
+            dst_ref=arrived.at[e, pl.ds(dst, size)],
             send_sem=wave_out.at[e, h],
             recv_sem=wave_in.at[e, h],
             device_id=(partner[e], group),
             device_id_type=MESH,
         )
+
+    last = HALVES * CHUNK - LEFT_OUT
+
+    def wave(e, h):
+        if e < 2:
+            if h < HALVES:
+                return copy(e, h, sent + h * CHUNK, h * CHUNK, CHUNK)
+            return copy(e, h, worked + last, last + CHUNK, LEFT_OUT)
+        if h == 0:
+            return copy(e, h, worked, 0, CHUNK)
+        if h == 1:
+            return copy(e, h, worked + CHUNK, CHUNK, CHUNK - LEFT_OUT)
+        if h == 2:
+            return copy(e, h, worked + last, last, LEFT_OUT)
+        return copy(e, h, sent + last, last + CHUNK, LEFT_OUT)
 
     def listing(e):
         return pltpu.make_async_remote_copy(
@@ -151,9 +170,9 @@
         )
 
     def send(e):
+        listing(e).start()
         for h in range(HALVES):
             wave(e, h).start()
-        listing(e).start()
 
     @pl.when(late == 0)
     def _():
@@ -164,12 +183,18 @@
         pl.semaphore_wait(barrier, 6)
         greet(ready, (partner[2], group))
         send(2)
+        wave(2, 2).start()
+        wave(2, 3).start()
 
     send(1)
     send(0)
 
+    @pl.when(late == 0)
+    def _():
+        wave(1, 2).start()
+
     loads[1].wait()
-    spectra[0] = jnp.dot(
+    spectra[0, : HALVES * CHUNK] = jnp.dot(
         normal[pl.ds(pl.multiple_of(worked, CHUNK), HALVES * CHUNK)], forward[...], preferred_element_type=jnp.float32
     ).astype(jnp.bfloat16)
     loads[2].wait()
@@ -196,18 +221,45 @@
             event = jnp.concatenate([event] * COMP, axis=0)
             picks[side] = jnp.where(cell == part + event, 1.0, 0.0).astype(jnp.bfloat16)
         total[...] = jnp.zeros_like(total)
-
-        @pl.loop(0, HALVES)
+        known = 2 if e == 2 else 0
+
+        def pick_left(h):
+            left[h] = jnp.dot(picks[0], spectra[known, h * CHUNK : (h + 1) * CHUNK], preferred_element_type=jnp.float32)
+
+        for h in range(HALVES):
+            pick_left(h)
+        if e == 2:
+
+            @pl.when(late == 0)
+            def _():
+                wave(1, 2).wait_recv()
+                spectra[2, HALVES * CHUNK :] = jnp.dot(
+                    arrived[1, HALVES * CHUNK :], forward[...], preferred_element_type=jnp.float32
+                ).astype(jnp.bfloat16)
+                pick_left(2)
+
+        @pl.loop(0, HALVES + 1 - late if e == 2 else HALVES)
         def _(h):
-            wave(e, h).wait_recv()
+            for k in range(HALVES):
+
+                @pl.when(h == k)
+                def _(k=k):
+                    wave(e, k).wait_recv()
+
+            if e == 2:
+                for k in range(HALVES):
+
+                    @pl.when((late == 0) & (h == k + 1))
+                    def _(k=k):
+                        wave(2, k + 2).wait_recv()
+
             spectra[1 + e, rows(0, h)] = jnp.dot(
                 arrived[e, rows(0, h)], forward[...], preferred_element_type=jnp.float32
             ).astype(jnp.bfloat16)
-            left[...] = jnp.dot(picks[0], spectra[e if e == 2 else 0, rows(0, h)], preferred_element_type=jnp.float32)
             right[...] = jnp.dot(picks[1], spectra[1 + e, rows(0, h)], preferred_element_type=jnp.float32)
             for c in range(COMP):
                 at = pl.ds(c * 2 * SLOTS, 2 * SLOTS)
-                lr, li, lm = left[at, 0:256], left[at, 256:512], left[at, 512:640]
+                lr, li, lm = left[h, at, 0:256], left[h, at, 256:512], left[h, at, 512:640]
                 rr, ri, rm = right[at, 0:256], right[at, 256:512], right[at, 512:640]
                 total[:, 0:256] += lr * rr + li * ri
                 total[:, 256:512] += lr * ri - li * rr
@@ -260,6 +312,19 @@
         listing(e).wait_send()
         for h in range(HALVES):
             wave(e, h).wait_send()
+        if e == 1:
+
+            @pl.when(late == 0)
+            def _():
+                wave(1, 2).wait_send()
+
+        if e == 2:
+
+            @pl.when(late == 1)
+            def _():
+                wave(2, 2).wait_send()
+                wave(2, 3).wait_send()
+
         for side in range(2):
             for d in range(GROUP):
                 if e == 2 or side == 1 or d > 0:
@@ -288,9 +353,9 @@
             pltpu.VMEM((LENGTH, PERIOD), bf16),
             pltpu.VMEM((WIDE, LAGS), bf16),
             pltpu.VMEM((TRACES, LENGTH), bf16),
-            pltpu.VMEM((ROUNDS, HALVES * CHUNK, LENGTH), bf16),
-            pltpu.VMEM((1 + ROUNDS, HALVES * CHUNK, PERIOD), bf16),
-            pltpu.VMEM((COMP * 2 * SLOTS, PERIOD), f32),
+            pltpu.VMEM((ROUNDS, (HALVES + 1) * CHUNK, LENGTH), bf16),
+            pltpu.VMEM((1 + ROUNDS, (HALVES + 1) * CHUNK, PERIOD), bf16),
+            pltpu.VMEM((HALVES + 1, COMP * 2 * SLOTS, PERIOD), f32),
             pltpu.VMEM((COMP * 2 * SLOTS, PERIOD), f32),
             pltpu.VMEM((2 * SLOTS, WIDE), f32),
             pltpu.VMEM((8, 128), jnp.int32),
@@ -299,8 +364,8 @@
             pltpu.VMEM((ROUNDS, 2 * GROUP, 16, 128), bf16),
             pltpu.VMEM((ROUNDS, 2 * GROUP, 16, 128), bf16),
             dma((5,)),
-            dma((ROUNDS, HALVES)),
-            dma((ROUNDS, HALVES)),
+            dma((ROUNDS, 2 * HALVES)),
+            dma((ROUNDS, 2 * HALVES)),
             dma((ROUNDS,)),
             dma((ROUNDS,)),
             dma((ROUNDS, 2 * GROUP)),

time: 23.9 us -> 22.7 us (0.950)
  Pallas kernels: 22.5 us -> 21.2 us
    pallas_call x1, Pallas kernels: 22.5 us -> 21.2 us  [shards(): pl.pallas_call(kernel, out_shape=jax.ShapeDtypeStruct((ROUNDS, 8, LAGS),...]
where the time goes in v4:
time: 22.7 us; the launch traced here: 22.6 us
  Pallas kernels  21.2 us (93%)
  local copies, waits for them, and re-layouts  1.3 us (6%)
    pallas_call x1, Pallas kernels, shards(): pl.pallas_call(kernel, out_shape=jax.ShapeDtypeStruct((ROUNDS, 8, LAGS),...  21.2 us
    unnamed x5, local copies, waits for them, and re-layouts  1.3 us

profile of v4, /device:TPU:1, one launch (start us, length us, event | category | flops | bytes accessed | tf_op | source)
XLA Modules:
  0.0 22.6 jit_solution(17743856684579545555)
XLA Ops:
  0.0 0.0 copy-start
  0.0 0.0 copy-start.1
  0.0 0.7 %copy-done = s32[3,32,2]{1,2,0:T(2,128)S(1)} copy-done((s32[3,32,2]{1,2,0:T(2,128)S(1)}, s32[3,32,2]{1,2,0:T(2,128)}, u32[]{:S(2)}) %copy-start) | copy-done | bytes 792
  0.7 0.0 copy-done.1
  0.7 21.2 %correlate.1 = f32[3,8,256]{2,1,0:T(8,128)S(1)} custom-call(bf16[16,3,4,512]{3,2,1,0:T(4,128)(2,1)} %bitcast.5, s32[3,2,32]{2,1,0:T(2,128)S(1)} %bitcast.3, s32[1,3]{1,0:T(1,128)S(1)} %bitcast.4, bf16[512,640]{1,0:T(8,128)(2,1)} %constant.4.clone.forward_hbm, bf16[768,256]{1,0:T(8,128)(2,1)} %constant.5.clone.inverse_hbm), custom_call_target="tpu_custom_call" | custom-call | tf_op jit(solution)/shard_map/correlate/pallas_call | solution.py:338
  21.9 0.6 %copy.7 = f32[3,8,256]{2,1,0:T(8,128)} copy(f32[3,8,256]{2,1,0:T(8,128)S(1)} %correlate.1) | data formatting | bytes 49152
Async XLA Ops:
  0.0 0.7 %copy-start = (s32[3,32,2]{1,2,0:T(2,128)S(1)}, s32[3,32,2]{1,2,0:T(2,128)}, u32[]{:S(2)}) copy-start(s32[3,32,2]{1,2,0:T(2,128)} %param.6) | copy-start | bytes 2308
  0.0 0.7 %copy-start.1 = (s32[3,1]{0,1:T(1,128)S(1)}, s32[3,1]{0,1:T(1,128)}, u32[]{:S(2)}) copy-start(s32[3,1]{0,1:T(1,128)} %param.7) | copy-start | bytes 40

commit v5 on v4

--- a/solution.py
+++ b/solution.py
@@ -97,14 +97,14 @@
     turned = jnp.where(even, pltpu.roll(turned, 7, 0), pltpu.roll(turned, 1, 0))
     message[...] = mine + turned
 
+    row = lax.broadcasted_iota(jnp.int32, (TRACES, TRACES), 0)
+    column = lax.broadcasted_iota(jnp.int32, (TRACES, TRACES), 1)
+    source = lax.rem(row, EVENTS) * (COMP * GROUP) + lax.rem(row // EVENTS, COMP) * GROUP + row // CHUNK
+    reorder = jnp.where(column == source, 1.0, 0.0).astype(jnp.bfloat16)
     loads[0].wait()
     traces = x_in[...].astype(jnp.float32).reshape(TRACES, LENGTH)
     traces = traces - jnp.mean(traces, axis=-1, keepdims=True)
     traces = traces * lax.rsqrt(jnp.mean(traces * traces, axis=-1, keepdims=True) + EPS)
-    row = lax.broadcasted_iota(jnp.int32, (TRACES, TRACES), 0)
-    column = lax.broadcasted_iota(jnp.int32, (TRACES, TRACES), 1)
-    source = lax.rem(row, EVENTS) * (COMP * GROUP) + lax.rem(row // EVENTS, COMP) * GROUP + row // CHUNK
-    reorder = jnp.where(column == source, 1.0, 0.0).astype(jnp.bfloat16)
     normal[...] = jnp.dot(
         reorder, traces.astype(jnp.bfloat16), preferred_element_type=jnp.float32
     ).astype(jnp.bfloat16)
@@ -152,20 +152,20 @@
         return pltpu.make_async_remote_copy(
             src_ref=shares.at[e, GROUP * side + mates[d]],
             dst_ref=gathered.at[e, GROUP * side + group],
-            send_sem=share_out.at[e, GROUP * side + mates[d]],
-            recv_sem=share_in.at[e, GROUP * side + group],
+            send_sem=share_out.at[e],
+            recv_sem=share_in.at[e],
             device_id=(to, mates[d]),
             device_id_type=MESH,
         )
 
-    def landed(e, side, d):
-        to = partner[e] if side == 1 else partner[1] if e == 2 else region
+    def all_shares(e):
+        size = 2 * GROUP if e == 2 else 2 * GROUP - 1
         return pltpu.make_async_remote_copy(
-            src_ref=shares.at[e, GROUP * side + mates[d]],
-            dst_ref=gathered.at[e, GROUP * side + mates[d]],
-            send_sem=share_out.at[e, GROUP * side + mates[d]],
-            recv_sem=share_in.at[e, GROUP * side + mates[d]],
-            device_id=(to, mates[d]),
+            src_ref=shares.at[e, pl.ds(0, size)],
+            dst_ref=gathered.at[e, pl.ds(0, size)],
+            send_sem=share_out.at[e],
+            recv_sem=share_in.at[e],
+            device_id=(partner[e], group),
             device_id_type=MESH,
         )
 
@@ -257,14 +257,18 @@
                 arrived[e, rows(0, h)], forward[...], preferred_element_type=jnp.float32
             ).astype(jnp.bfloat16)
             right[...] = jnp.dot(picks[1], spectra[1 + e, rows(0, h)], preferred_element_type=jnp.float32)
-            for c in range(COMP):
-                at = pl.ds(c * 2 * SLOTS, 2 * SLOTS)
-                lr, li, lm = left[h, at, 0:256], left[h, at, 256:512], left[h, at, 512:640]
-                rr, ri, rm = right[at, 0:256], right[at, 256:512], right[at, 512:640]
-                total[:, 0:256] += lr * rr + li * ri
-                total[:, 256:512] += lr * ri - li * rr
-                total[:, 512:640] += lm * rm
-                total[:, 640:768] += lm * pltpu.roll(rm, 64, 1)
+            for g in range(2 * SLOTS // 16):
+                to = pl.ds(16 * g, 16)
+                sums = [total[to, 0:256], total[to, 256:512], total[to, 512:640], total[to, 640:768]]
+                for c in range(COMP):
+                    at = pl.ds(c * 2 * SLOTS + 16 * g, 16)
+                    lr, li, lm = left[h, at, 0:256], left[h, at, 256:512], left[h, at, 512:640]
+                    rr, ri, rm = right[at, 0:256], right[at, 256:512], right[at, 512:640]
+                    sums[0] += lr * rr + li * ri
+                    sums[1] += lr * ri - li * rr
+                    sums[2] += lm * rm
+                    sums[3] += lm * pltpu.roll(rm, 64, 1)
+                total[to, 0:256], total[to, 256:512], total[to, 512:640], total[to, 640:768] = sums
 
         real, imag, both, cross = total[:, 0:256], total[:, 256:512], total[:, 512:640], total[:, 640:768]
         imag = jnp.where(theirs_row, -imag, imag)
@@ -297,38 +301,31 @@
     def _():
         work(0)
 
+    for e in range(ROUNDS):
+        listing(e).wait_send()
+        for h in range(HALVES):
+            wave(e, h).wait_send()
+
+    @pl.when(late == 0)
+    def _():
+        wave(1, 2).wait_send()
+
+    @pl.when(late == 1)
+    def _():
+        wave(2, 2).wait_send()
+        wave(2, 3).wait_send()
+
+
     slot = group * 8 + lax.rem(lax.broadcasted_iota(jnp.int32, (16, 128), 0), 8)
     for e in range(ROUNDS):
-        for side in range(2):
-            for d in range(GROUP):
-                if e == 2 or side == 1 or d > 0:
-                    landed(e, side, d).wait_recv()
+        all_shares(e).wait_recv()
         curve = jnp.sum(gathered[e].astype(jnp.float32), axis=0)
         curve = jnp.where(slot < counts_ref[0, e], curve, 0.0)
         out_ref[e, :, 0:128] = curve[0:8]
         out_ref[e, :, 128:256] = curve[8:16]
 
     for e in range(ROUNDS):
-        listing(e).wait_send()
-        for h in range(HALVES):
-            wave(e, h).wait_send()
-        if e == 1:
-
-            @pl.when(late == 0)
-            def _():
-                wave(1, 2).wait_send()
-
-        if e == 2:
-
-            @pl.when(late == 1)
-            def _():
-                wave(2, 2).wait_send()
-                wave(2, 3).wait_send()
-
-        for side in range(2):
-            for d in range(GROUP):
-                if e == 2 or side == 1 or d > 0:
-                    share(e, side, d).wait_send()
+        all_shares(e).wait_send()
 
 
 def shards(waveforms, pair_lists, pair_counts):
@@ -368,8 +365,8 @@
             dma((ROUNDS, 2 * HALVES)),
             dma((ROUNDS,)),
             dma((ROUNDS,)),
-            dma((ROUNDS, 2 * GROUP)),
-            dma((ROUNDS, 2 * GROUP)),
+            dma((ROUNDS,)),
+            dma((ROUNDS,)),
             pltpu.SemaphoreType.REGULAR,
             pltpu.SemaphoreType.REGULAR,
         ],
@@ -379,8 +376,8 @@
         name="correlate",
     )(
         jnp.transpose(waveforms, (0, 2, 1, 3)),
-        jnp.transpose(pair_lists, (0, 2, 1)),
-        jnp.transpose(pair_counts, (1, 0)),
+        pltpu.with_memory_space_constraint(jnp.transpose(pair_lists, (0, 2, 1)), pltpu.HBM),
+        pltpu.with_memory_space_constraint(jnp.transpose(pair_counts, (1, 0)), pltpu.HBM),
         jnp.asarray(forward),
         jnp.asarray(inverse),
     )

time: 22.7 us -> 21.8 us (0.960)
  local copies, waits for them, and re-layouts: 1.3 us -> 0.61 us
    unnamed x5 -> x1, local copies, waits for them, and re-layouts: 1.3 us -> 0.61 us
where the time goes in v5:
time: 21.8 us; the launch traced here: 21.7 us
  Pallas kernels  21 us (96%)
  local copies, waits for them, and re-layouts  0.61 us (3%)
    pallas_call x1, Pallas kernels, shards(): pl.pallas_call(kernel, out_shape=jax.ShapeDtypeStruct((ROUNDS, 8, LAGS),...  21 us
    unnamed x1, local copies, waits for them, and re-layouts  0.61 us

profile of v5, /device:TPU:1, one launch (start us, length us, event | category | flops | bytes accessed | tf_op | source)
XLA Modules:
  0.0 21.7 jit_solution(14520371608158106618)
XLA Ops:
  0.0 21.0 %correlate.1 = f32[3,8,256]{2,1,0:T(8,128)S(1)} custom-call(bf16[16,3,4,512]{3,2,1,0:T(4,128)(2,1)} %bitcast.3, s32[3,2,32]{2,1,0:T(2,128)} %bitcast.4, s32[1,3]{1,0:T(1,128)} %bitcast.5, bf16[512,640]{1,0:T(8,128)(2,1)} %constant.4.clone.forward_hbm, bf16[768,256]{1,0:T(8,128)(2,1)} %constant.5.clone.inverse_hbm), custom_call_target="tpu_custom_call" | custom-call | tf_op jit(solution)/shard_map/correlate/pallas_call | solution.py:335
  21.1 0.6 %copy.7 = f32[3,8,256]{2,1,0:T(8,128)} copy(f32[3,8,256]{2,1,0:T(8,128)S(1)} %correlate.1) | data formatting | bytes 49152

commit v6 on v5

--- a/solution.py
+++ b/solution.py
@@ -84,8 +84,8 @@
         pltpu.make_async_copy(lists_hbm, lists_ref, load_sem.at[3]),
         pltpu.make_async_copy(counts_hbm, counts_ref, load_sem.at[4]),
     ]
-    for load in loads:
-        load.start()
+    for k in (3, 0, 1, 2, 4):
+        loads[k].start()
 
     loads[3].wait()
     message[...] = jnp.zeros_like(message)
@@ -238,25 +238,11 @@
                 ).astype(jnp.bfloat16)
                 pick_left(2)
 
-        @pl.loop(0, HALVES + 1 - late if e == 2 else HALVES)
-        def _(h):
-            for k in range(HALVES):
-
-                @pl.when(h == k)
-                def _(k=k):
-                    wave(e, k).wait_recv()
-
-            if e == 2:
-                for k in range(HALVES):
-
-                    @pl.when((late == 0) & (h == k + 1))
-                    def _(k=k):
-                        wave(2, k + 2).wait_recv()
-
-            spectra[1 + e, rows(0, h)] = jnp.dot(
-                arrived[e, rows(0, h)], forward[...], preferred_element_type=jnp.float32
+        def unit(h):
+            spectra[1 + e, h * CHUNK : (h + 1) * CHUNK] = jnp.dot(
+                arrived[e, h * CHUNK : (h + 1) * CHUNK], forward[...], preferred_element_type=jnp.float32
             ).astype(jnp.bfloat16)
-            right[...] = jnp.dot(picks[1], spectra[1 + e, rows(0, h)], preferred_element_type=jnp.float32)
+            right[...] = jnp.dot(picks[1], spectra[1 + e, h * CHUNK : (h + 1) * CHUNK], preferred_element_type=jnp.float32)
             for g in range(2 * SLOTS // 16):
                 to = pl.ds(16 * g, 16)
                 sums = [total[to, 0:256], total[to, 256:512], total[to, 512:640], total[to, 640:768]]
@@ -269,6 +255,22 @@
                     sums[2] += lm * rm
                     sums[3] += lm * pltpu.roll(rm, 64, 1)
                 total[to, 0:256], total[to, 256:512], total[to, 512:640], total[to, 640:768] = sums
+
+        for h in range(HALVES):
+            wave(e, h).wait_recv()
+            if e == 2 and h == 1:
+
+                @pl.when(late == 0)
+                def _():
+                    wave(2, 2).wait_recv()
+
+            unit(h)
+        if e == 2:
+
+            @pl.when(late == 0)
+            def _():
+                wave(2, 3).wait_recv()
+                unit(2)
 
         real, imag, both, cross = total[:, 0:256], total[:, 256:512], total[:, 512:640], total[:, 640:768]
         imag = jnp.where(theirs_row, -imag, imag)

time: 21.8 us -> 21.5 us (0.986)
    pallas_call x1, Pallas kernels: 21 us -> 20.8 us  [shards(): pl.pallas_call(kernel, out_shape=jax.ShapeDtypeStruct((ROUNDS, 8, LAGS),...]
where the time goes in v6:
time: 21.5 us; the launch traced here: 21.4 us
  Pallas kernels  20.8 us (97%)
  local copies, waits for them, and re-layouts  0.61 us (3%)
    pallas_call x1, Pallas kernels, shards(): pl.pallas_call(kernel, out_shape=jax.ShapeDtypeStruct((ROUNDS, 8, LAGS),...  20.8 us
    unnamed x1, local copies, waits for them, and re-layouts  0.61 us

profile of v6, /device:TPU:1, one launch (start us, length us, event | category | flops | bytes accessed | tf_op | source)
XLA Modules:
  0.0 21.4 jit_solution(6588856912032809371)
XLA Ops:
  0.0 20.8 %correlate.1 = f32[3,8,256]{2,1,0:T(8,128)S(1)} custom-call(bf16[16,3,4,512]{3,2,1,0:T(4,128)(2,1)} %bitcast.3, s32[3,2,32]{2,1,0:T(2,128)} %bitcast.4, s32[1,3]{1,0:T(1,128)} %bitcast.5, bf16[512,640]{1,0:T(8,128)(2,1)} %constant.4.clone.forward_hbm, bf16[768,256]{1,0:T(8,128)(2,1)} %constant.5.clone.inverse_hbm), custom_call_target="tpu_custom_call" | custom-call | tf_op jit(solution)/shard_map/correlate/pallas_call | solution.py:337
  20.8 0.6 %copy.7 = f32[3,8,256]{2,1,0:T(8,128)} copy(f32[3,8,256]{2,1,0:T(8,128)S(1)} %correlate.1) | data formatting | bytes 49152

commit v7 on v6

--- a/solution.py
+++ b/solution.py
@@ -148,7 +148,8 @@
         )
 
     def share(e, side, d):
-        to = partner[e] if side == 1 else partner[1] if e == 2 else region
+        near = partner[1] if e == 2 else region
+        to = near + side * (partner[e] - near)
         return pltpu.make_async_remote_copy(
             src_ref=shares.at[e, GROUP * side + mates[d]],
             dst_ref=gathered.at[e, GROUP * side + group],
@@ -272,21 +273,41 @@
                 wave(2, 3).wait_recv()
                 unit(2)
 
-        real, imag, both, cross = total[:, 0:256], total[:, 256:512], total[:, 512:640], total[:, 640:768]
-        imag = jnp.where(theirs_row, -imag, imag)
-        cross = jnp.where(theirs_row[:, :128], -cross, cross)
-        curves = jnp.dot(
-            jnp.concatenate([real, imag, both, cross], axis=1).astype(jnp.bfloat16),
-            inverse[...],
-            preferred_element_type=jnp.float32,
-        )
-        for k in range(2 * GROUP):
-            piece = curves[8 * k : 8 * k + 8]
-            shares[e, k] = jnp.concatenate([piece[:, :128], piece[:, 128:]], axis=0).astype(jnp.bfloat16)
-        for side in range(2):
-            for d in range(GROUP):
-                if e == 2 or side == 1 or d > 0:
-                    share(e, side, d).start()
+        if e == 2:
+            for turn in range(2):
+                side = 1 - late if turn else late
+                half = pl.ds(pl.multiple_of(side * SLOTS, SLOTS), SLOTS)
+                sign = (1 - 2 * side) * jnp.ones((SLOTS, LAGS), jnp.float32)
+                real, imag, both, cross = total[half, 0:256], total[half, 256:512], total[half, 512:640], total[half, 640:768]
+                curves = jnp.dot(
+                    jnp.concatenate([real, imag * sign, both, cross * sign[:, :128]], axis=1).astype(jnp.bfloat16),
+                    inverse[...],
+                    preferred_element_type=jnp.float32,
+                )
+                for k in range(GROUP):
+                    piece = curves[8 * k : 8 * k + 8]
+                    shares[e, GROUP * side + k] = jnp.concatenate([piece[:, :128], piece[:, 128:]], axis=0).astype(jnp.bfloat16)
+                for d in range(GROUP):
+                    if e == 2 or turn == 0 or d > 0:
+                        share(e, side, d).start()
+
+        else:
+            real, imag, both, cross = total[:, 0:256], total[:, 256:512], total[:, 512:640], total[:, 640:768]
+            imag = jnp.where(theirs_row, -imag, imag)
+            cross = jnp.where(theirs_row[:, :128], -cross, cross)
+            curves = jnp.dot(
+                jnp.concatenate([real, imag, both, cross], axis=1).astype(jnp.bfloat16),
+                inverse[...],
+                preferred_element_type=jnp.float32,
+            )
+            for k in range(2 * GROUP):
+                piece = curves[8 * k : 8 * k + 8]
+                shares[e, k] = jnp.concatenate([piece[:, :128], piece[:, 128:]], axis=0).astype(jnp.bfloat16)
+            for side in range(2):
+                for d in range(GROUP):
+                    if e == 2 or side == 1 or d > 0:
+                        share(e, side, d).start()
+
         if e < 2:
             gathered[e, pl.ds(group, 1)] = shares[e, pl.ds(group, 1)]
 

time: 21.5 us -> 21.5 us (level)
  no operation moved by 1% of the time
where the time goes in v7:
time: 21.5 us; the launch traced here: 21.4 us
  Pallas kernels  20.8 us (97%)
  local copies, waits for them, and re-layouts  0.61 us (3%)
    pallas_call x1, Pallas kernels, shards(): pl.pallas_call(kernel, out_shape=jax.ShapeDtypeStruct((ROUNDS, 8, LAGS),...  20.8 us
    unnamed x1, local copies, waits for them, and re-layouts  0.61 us

profile of v7, /device:TPU:1, one launch (start us, length us, event | category | flops | bytes accessed | tf_op | source)
XLA Modules:
  0.0 21.4 jit_solution(3765514789311924763)
XLA Ops:
  0.0 20.8 %correlate.1 = f32[3,8,256]{2,1,0:T(8,128)S(1)} custom-call(bf16[16,3,4,512]{3,2,1,0:T(4,128)(2,1)} %bitcast.3, s32[3,2,32]{2,1,0:T(2,128)} %bitcast.4, s32[1,3]{1,0:T(1,128)} %bitcast.5, bf16[512,640]{1,0:T(8,128)(2,1)} %constant.4.clone.forward_hbm, bf16[768,256]{1,0:T(8,128)(2,1)} %constant.5.clone.inverse_hbm), custom_call_target="tpu_custom_call" | custom-call | tf_op jit(solution)/shard_map/correlate/pallas_call | solution.py:358
  20.8 0.6 %copy.7 = f32[3,8,256]{2,1,0:T(8,128)} copy(f32[3,8,256]{2,1,0:T(8,128)S(1)} %correlate.1) | data formatting | bytes 49152
